TPU v7x, 32 devices: a whole 2x2x4 slice. The times are simulated.
32 devices in a mesh: dp: 8 (over z, x), group: 4 (over y, core).
Axes of the slice: x: 2, y: 2, z: 4, core: 2. Of those that a mesh axis runs over, the one named last changes fastest.
Arguments:
- tokens_in: bfloat16 [16384, 768], P(('dp', 'group')), may hold values from -6 to 6
- cotangent: float32 [16384, 768], P(('dp', 'group')), may hold values from -6 to 6
- seq_lengths: int32 [32], P(('dp', 'group')), may hold values from 128 to 512, as said below
- drop_order: int32 [32, 512], P(('dp', 'group')), may hold values from 0 to 511, each once within a row
- routes: int32 [2, 16384, 2], P(None, ('dp', 'group')), may hold values from 0 to 7, all different within a row
- dense_master: float32 [4751360], P(('dp', 'group'))
- dense_moment: float32 [4751360], P(('dp', 'group')), may hold values from -0.00030517578 to 0.00030517578
- dense_second: float32 [4751360], P(('dp', 'group')), may hold values from 1e-09 to 1e-08
- expert_master: float32 [4, 2, 3, 2048, 768], P('group', None, None, 'dp')
- expert_moment: float32 [4, 2, 3, 2048, 768], P('group', None, None, 'dp'), may hold values from -0.00030517578 to 0.00030517578
- expert_second: float32 [4, 2, 3, 2048, 768], P('group', None, None, 'dp'), may hold values from 1e-09 to 1e-08
Outputs:
- output: bfloat16 [16384, 768], P(('dp', 'group'))
- grad_input: float32 [16384, 768], P(('dp', 'group'))
- dense_grad: float32 [4751360], P(('dp', 'group'))
- expert_grad: float32 [4, 2, 3, 2048, 768], P('group', None, None, 'dp')
- gain_grad: float32 [2, 2, 768], replicated
- dense_step: float32 [4751360], P(('dp', 'group'))
- expert_step: float32 [4, 2, 3, 2048, 768], P('group', None, None, 'dp')
Inputs may be any that keep to these rules, and one draw needn't show every extreme that they name: `seq_lengths`: one device holds a sequence of 512 tokens. `drop_order`: each device's row is a permutation. `routes`: the two ids of a token differ; ids below 4 are feed-forward experts, 4 the zero expert, 5 the copy expert, the last two constant experts.
All inputs are finite; a program needn't handle non-finite values.
Results may differ from a plain program's by a relative error of at most 0.022.
Values may be sent and summed in bfloat16 or wider, within the bound.
No kernel may reach another device: no remote copies, remote signals or barrier semaphores. Data moves between devices by JAX's collectives and lax.ppermute only.
A program may use at most 256 MiB of HBM per device.

v0:
```python
import jax
import jax.numpy as jnp
from jax import lax
from jax.sharding import PartitionSpec as P

HEADS = 12
LAYERS = 2


norm_eps = 1e-06
rope_base = 10000.0
neg_big = -1e30
adam_rate = 0.001
beta_one = 0.9
beta_two = 0.95
adam_eps = 1e-08
decay_rate = 0.1
clip_norm = 1.0
step_number = 10
highest = lax.Precision.HIGHEST


def layout(width, routed):
    items = []
    for depth in range(LAYERS):
        items = items + [
            (depth, "query", (width, width)),
            (depth, "key", (width, width)),
            (depth, "value", (width, width)),
            (depth, "output", (width, width)),
            (depth, "router", (width, routed)),
            (depth, "mixing", (width, 4)),
            (depth, "constant", (2, width)),
            (depth, "attn_gain", (width,)),
            (depth, "moe_gain", (width,)),
        ]
        if depth > 0:
            items.append((depth, "carry", (routed, routed)))
    return items


def unpack(flat, width, routed):
    params = [dict() for depth in range(LAYERS)]
    cursor = 0
    for depth, name, shape in layout(width, routed):
        amount = 1
        for extent in shape:
            amount = amount * extent
        params[depth][name] = flat[cursor : cursor + amount].reshape(shape)
        cursor = cursor + amount
    return params


def pack(grads, width, routed, whole_size):
    pieces = [grads[depth][name].reshape(-1) for depth, name, shape in layout(width, routed)]
    flat = jnp.concatenate(pieces)
    return jnp.concatenate([flat, jnp.zeros((whole_size - flat.shape[0],), jnp.float32)])


def rms_forward(stream, gain):
    inverse = lax.rsqrt(jnp.mean(stream * stream, axis=-1, keepdims=True) + norm_eps)
    return (stream * inverse * gain, inverse)


def rms_backward(stream, inverse, gain, grad_normed):
    grad_gain = jnp.sum(grad_normed * stream * inverse, axis=0)
    scaled = grad_normed * gain
    inner = jnp.mean(stream * scaled, axis=-1, keepdims=True)
    return (inverse * scaled - stream * (inverse * inverse * inverse) * inner, grad_gain)


def rope_tables(count, half):
    position = jnp.arange(count, dtype=jnp.float32)[:, None]
    frequency = rope_base ** (-jnp.arange(half, dtype=jnp.float32) / half)
    angle = position * frequency[None, :]
    return (jnp.cos(angle)[:, None, :], jnp.sin(angle)[:, None, :])


def rotate(values, cosine, sine):
    half = values.shape[-1] // 2
    first, second = (values[..., :half], values[..., half:])
    return jnp.concatenate(
        [first * cosine - second * sine, second * cosine + first * sine], axis=-1
    )


def rotate_back(grads, cosine, sine):
    half = grads.shape[-1] // 2
    first, second = (grads[..., :half], grads[..., half:])
    return jnp.concatenate(
        [first * cosine + second * sine, second * cosine - first * sine], axis=-1
    )


def visible(first, block, count, length):
    rows = first + jnp.arange(block)[:, None]
    cols = jnp.arange(count)[None, :]
    return (cols <= rows) & (cols < length)


def assign_slots(routes_now, order, length, experts, capacity):
    count = order.shape[0]
    live = jnp.arange(count) < length
    which = jnp.arange(experts)
    hits = (routes_now[:, :, None] == which[None, None, :]) & live[:, None, None]
    marks = jnp.sum(hits.astype(jnp.int32), axis=1).astype(jnp.bfloat16)
    earlier = (order[None, :] < order[:, None]).astype(jnp.bfloat16)
    ranks = jnp.dot(earlier, marks, preferred_element_type=jnp.float32).astype(jnp.int32)
    rank_pick = jnp.sum(jnp.where(hits, ranks[:, None, :], 0), axis=2)
    kept = jnp.any(hits, axis=2) & (rank_pick < capacity)
    return jnp.where(kept, routes_now * capacity + rank_pick, experts * capacity)


def attend(queries, keys, values, length, block):
    count = queries.shape[0]
    scale = queries.shape[2] ** (-0.5)
    scores = jnp.einsum("qhd,khd->hqk", queries, keys, preferred_element_type=jnp.float32) * scale
    scores = jnp.where(visible(0, block, count, length)[None], scores, neg_big)
    peak = jnp.max(scores, axis=-1, keepdims=True)
    weights = jnp.exp(scores - peak)
    total = jnp.sum(weights, axis=-1, keepdims=True)
    probs = (weights / total).astype(jnp.bfloat16)
    outputs = jnp.einsum("hqk,khd->qhd", probs, values, preferred_element_type=jnp.float32)
    totals = peak + jnp.log(total)
    return (outputs, totals)


def attend_back(queries, keys, values, logsum, grad_out, length, block):
    count = queries.shape[0]
    scale = queries.shape[2] ** (-0.5)
    grad_query_parts = []
    grad_keys = jnp.zeros(keys.shape, jnp.float32)
    grad_values = jnp.zeros(values.shape, jnp.float32)
    for first in range(0, count, block):
        rows = queries[first : first + block]
        grad_rows = grad_out[first : first + block]
        scores = jnp.einsum("qhd,khd->hqk", rows, keys, preferred_element_type=jnp.float32) * scale
        scores = jnp.where(visible(first, block, count, length)[None], scores, neg_big)
        probs = jnp.exp(scores - logsum[:, first : first + block])
        grad_probs = jnp.einsum(
            "qhd,khd->hqk", grad_rows, values, preferred_element_type=jnp.float32
        )
        inner = jnp.sum(probs * grad_probs, axis=-1, keepdims=True)
        grad_scores = (probs * (grad_probs - inner)).astype(jnp.bfloat16)
        grad_query_parts.append(
            jnp.einsum("hqk,khd->qhd", grad_scores, keys, preferred_element_type=jnp.float32)
            * scale
        )
        grad_keys = (
            grad_keys
            + jnp.einsum("hqk,qhd->khd", grad_scores, rows, preferred_element_type=jnp.float32)
            * scale
        )
        grad_values = grad_values + jnp.einsum(
            "hqk,qhd->khd",
            probs.astype(jnp.bfloat16),
            grad_rows,
            preferred_element_type=jnp.float32,
        )
    return (jnp.concatenate(grad_query_parts, axis=0), grad_keys, grad_values)


def adam_delta(master, moment, second, grad):
    moment_new = beta_one * moment + (1.0 - beta_one) * grad
    second_new = beta_two * second + (1.0 - beta_two) * grad * grad
    fix_one = 1.0 - beta_one**step_number
    fix_two = 1.0 - beta_two**step_number
    direction = moment_new / fix_one / (jnp.sqrt(second_new / fix_two) + adam_eps)
    return adam_rate * (direction + decay_rate * master)


def on_device(
    tokens_in,
    cotangent,
    seq_lengths,
    drop_order,
    routes,
    dense_master,
    dense_moment,
    dense_second,
    expert_master,
    expert_moment,
    expert_second,
):
    count, width = tokens_in.shape
    heads = HEADS
    head_size = width // heads
    groups = lax.axis_size("group")
    routed = groups + 4
    capacity = max(2, 45 * count // (32 * routed))
    whole_size = dense_master.shape[0] * lax.axis_size(("dp", "group"))
    length = seq_lengths[0]
    order = drop_order[0]
    block = min(512, count)
    cosine, sine = rope_tables(count, head_size // 2)
    special = groups + jnp.arange(4)
    every_expert = jnp.arange(routed)
    dense_full = lax.all_gather(
        dense_master.astype(jnp.bfloat16), ("dp", "group"), axis=0, tiled=True
    )
    params = unpack(dense_full, width, routed)
    expert_full = lax.all_gather(expert_master.astype(jnp.bfloat16), "dp", axis=3, tiled=True)
    stream = tokens_in.astype(jnp.float32)
    carry_logits = jnp.zeros((count, routed), jnp.float32)
    saved = []
    for depth in range(LAYERS):
        weights = params[depth]
        route_now = routes[depth]
        slot = assign_slots(route_now, order, length, groups, capacity)
        attn_gain = weights["attn_gain"].astype(jnp.float32)
        normed, inverse = rms_forward(stream, attn_gain)
        normed_low = normed.astype(jnp.bfloat16)
        query = jnp.dot(normed_low, weights["query"], preferred_element_type=jnp.float32)
        keys = jnp.dot(normed_low, weights["key"], preferred_element_type=jnp.float32)
        values_low = (
            jnp.dot(normed_low, weights["value"], preferred_element_type=jnp.float32)
            .astype(jnp.bfloat16)
            .reshape(count, heads, head_size)
        )
        query_rot = rotate(query.reshape(count, heads, head_size), cosine, sine).astype(
            jnp.bfloat16
        )
        keys_rot = rotate(keys.reshape(count, heads, head_size), cosine, sine).astype(jnp.bfloat16)
        mixed, logsum = attend(query_rot, keys_rot, values_low, length, block)
        mixed_low = mixed.reshape(count, width).astype(jnp.bfloat16)
        middle = stream + jnp.dot(mixed_low, weights["output"], preferred_element_type=jnp.float32)
        moe_gain = weights["moe_gain"].astype(jnp.float32)
        normed_two, inverse_two = rms_forward(middle, moe_gain)
        normed_two_low = normed_two.astype(jnp.bfloat16)
        logits = jnp.dot(normed_two_low, weights["router"], preferred_element_type=jnp.float32)
        if depth > 0:
            logits = logits + jnp.dot(
                carry_logits, weights["carry"].astype(jnp.float32), precision=highest
            )
        chosen = jnp.take_along_axis(logits, route_now, axis=1)
        gates = jax.nn.softmax(chosen, axis=-1)
        send = (
            jnp.zeros((groups * capacity + 1, width), jnp.bfloat16)
            .at[slot.reshape(-1)]
            .set(jnp.repeat(normed_two_low, 2, axis=0))
        )
        arrived = lax.all_to_all(
            send[:-1].reshape(groups, capacity, width),
            "group",
            split_axis=0,
            concat_axis=0,
            tiled=True,
        ).reshape(groups * capacity, width)
        gate_w = expert_full[0, depth, 0]
        up_w = expert_full[0, depth, 1]
        down_w = expert_full[0, depth, 2]
        gate_value = jnp.einsum("rd,fd->rf", arrived, gate_w, preferred_element_type=jnp.float32)
        up_value = jnp.einsum("rd,fd->rf", arrived, up_w, preferred_element_type=jnp.float32)
        hidden = (jax.nn.silu(gate_value) * up_value).astype(jnp.bfloat16)
        expert_out = jnp.dot(hidden, down_w, preferred_element_type=jnp.float32).astype(
            jnp.bfloat16
        )
        returned = lax.all_to_all(
            expert_out.reshape(groups, capacity, width),
            "group",
            split_axis=0,
            concat_axis=0,
            tiled=True,
        ).reshape(groups * capacity, width)
        table = jnp.concatenate([returned, jnp.zeros((1, width), jnp.bfloat16)], axis=0)
        picked = table[slot].astype(jnp.float32)
        ffn_part = jnp.sum(gates[:, :, None] * picked, axis=1)
        special_hits = (route_now[:, :, None] == special[None, None, :]).astype(jnp.float32)
        special_gates = jnp.sum(gates[:, :, None] * special_hits, axis=1)
        mixing = weights["mixing"].astype(jnp.float32)
        mix_logits = jnp.dot(normed_two, mixing, precision=highest)
        mix_first = jax.nn.softmax(mix_logits[:, 0:2], axis=-1)
        mix_second = jax.nn.softmax(mix_logits[:, 2:4], axis=-1)
        constant = weights["constant"].astype(jnp.float32)
        constant_first = mix_first[:, 0:1] * normed_two + mix_first[:, 1:2] * constant[0]
        constant_second = mix_second[:, 0:1] * normed_two + mix_second[:, 1:2] * constant[1]
        routed_part = (
            ffn_part
            + special_gates[:, 1:2] * normed_two
            + special_gates[:, 2:3] * constant_first
            + special_gates[:, 3:4] * constant_second
        )
        saved.append(
            dict(
                stream_in=stream,
                inverse=inverse,
                attn_gain=attn_gain,
                normed_low=normed_low,
                query_rot=query_rot,
                keys_rot=keys_rot,
                values_low=values_low,
                logsum=logsum,
                mixed_low=mixed_low,
                middle=middle,
                inverse_two=inverse_two,
                moe_gain=moe_gain,
                normed_two=normed_two,
                normed_two_low=normed_two_low,
                carry_in=carry_logits,
                gates=gates,
                slot=slot,
                arrived=arrived,
                gate_value=gate_value,
                up_value=up_value,
                hidden=hidden,
                picked=picked,
                special_hits=special_hits,
                special_gates=special_gates,
                mixing=mixing,
                mix_first=mix_first,
                mix_second=mix_second,
                constant=constant,
                constant_first=constant_first,
                constant_second=constant_second,
            )
        )
        stream = middle + routed_part
        carry_logits = logits
    output = stream.astype(jnp.bfloat16)
    grad_stream = cotangent
    grad_carry = jnp.zeros((count, routed), jnp.float32)
    dense_grads = [None] * LAYERS
    expert_grads = [None] * LAYERS
    for depth in reversed(range(LAYERS)):
        weights = params[depth]
        held = saved[depth]
        route_now = routes[depth]
        slot = held["slot"]
        gates = held["gates"]
        normed_two = held["normed_two"]
        grad_moe = grad_stream
        grad_picked = gates[:, :, None] * grad_moe[:, None, :]
        grad_send = (
            jnp.zeros((groups * capacity + 1, width), jnp.bfloat16)
            .at[slot.reshape(-1)]
            .set(grad_picked.reshape(count * 2, width).astype(jnp.bfloat16))
        )
        grad_arrived = lax.all_to_all(
            grad_send[:-1].reshape(groups, capacity, width),
            "group",
            split_axis=0,
            concat_axis=0,
            tiled=True,
        ).reshape(groups * capacity, width)
        gate_w = expert_full[0, depth, 0]
        up_w = expert_full[0, depth, 1]
        down_w = expert_full[0, depth, 2]
        gate_value = held["gate_value"]
        sigmoid_gate = jax.nn.sigmoid(gate_value)
        grad_hidden = jnp.einsum(
            "rd,fd->rf", grad_arrived, down_w, preferred_element_type=jnp.float32
        )
        grad_up = (grad_hidden * gate_value * sigmoid_gate).astype(jnp.bfloat16)
        grad_gate = (
            grad_hidden
            * held["up_value"]
            * sigmoid_gate
            * (1.0 + gate_value * (1.0 - sigmoid_gate))
        ).astype(jnp.bfloat16)
        grad_down_w = jnp.einsum(
            "rf,rd->fd", held["hidden"], grad_arrived, preferred_element_type=jnp.float32
        )
        grad_gate_w = jnp.einsum(
            "rf,rd->fd", grad_gate, held["arrived"], preferred_element_type=jnp.float32
        )
        grad_up_w = jnp.einsum(
            "rf,rd->fd", grad_up, held["arrived"], preferred_element_type=jnp.float32
        )
        grad_rows = (
            jnp.einsum("rf,fd->rd", grad_gate, gate_w, preferred_element_type=jnp.float32)
            + jnp.einsum("rf,fd->rd", grad_up, up_w, preferred_element_type=jnp.float32)
        ).astype(jnp.bfloat16)
        grad_back = lax.all_to_all(
            grad_rows.reshape(groups, capacity, width),
            "group",
            split_axis=0,
            concat_axis=0,
            tiled=True,
        ).reshape(groups * capacity, width)
        grad_table = jnp.concatenate([grad_back, jnp.zeros((1, width), jnp.bfloat16)], axis=0)
        grad_from_experts = jnp.sum(grad_table[slot].astype(jnp.float32), axis=1)
        grad_gates = jnp.sum(grad_moe[:, None, :] * held["picked"], axis=2)
        zero_column = jnp.zeros((count,), jnp.float32)
        grad_special = jnp.stack(
            [
                zero_column,
                jnp.sum(grad_moe * normed_two, axis=1),
                jnp.sum(grad_moe * held["constant_first"], axis=1),
                jnp.sum(grad_moe * held["constant_second"], axis=1),
            ],
            axis=1,
        )
        grad_gates = grad_gates + jnp.sum(grad_special[:, None, :] * held["special_hits"], axis=2)
        grad_chosen = gates * (grad_gates - jnp.sum(gates * grad_gates, axis=1, keepdims=True))
        grad_logits = (
            jnp.sum(
                grad_chosen[:, :, None]
                * (route_now[:, :, None] == every_expert[None, None, :]).astype(jnp.float32),
                axis=1,
            )
            + grad_carry
        )
        router_w = weights["router"].astype(jnp.float32)
        grad_router = jnp.dot(
            held["normed_two_low"].astype(jnp.float32).T, grad_logits, precision=highest
        )
        grad_low_path = jnp.dot(grad_logits, router_w.T, precision=highest) + grad_from_experts
        layer_grads = dict()
        if depth > 0:
            layer_grads["carry"] = jnp.dot(held["carry_in"].T, grad_logits, precision=highest)
            grad_carry = jnp.dot(
                grad_logits, weights["carry"].astype(jnp.float32).T, precision=highest
            )
        special_gates = held["special_gates"]
        mix_first = held["mix_first"]
        mix_second = held["mix_second"]
        constant = held["constant"]
        grad_first = special_gates[:, 2:3] * grad_moe
        grad_second = special_gates[:, 3:4] * grad_moe
        grad_mix_first = jnp.stack(
            [jnp.sum(grad_first * normed_two, axis=1), jnp.sum(grad_first * constant[0], axis=1)],
            axis=1,
        )
        grad_mix_second = jnp.stack(
            [jnp.sum(grad_second * normed_two, axis=1), jnp.sum(grad_second * constant[1], axis=1)],
            axis=1,
        )
        grad_logit_first = mix_first * (
            grad_mix_first - jnp.sum(mix_first * grad_mix_first, axis=1, keepdims=True)
        )
        grad_logit_second = mix_second * (
            grad_mix_second - jnp.sum(mix_second * grad_mix_second, axis=1, keepdims=True)
        )
        grad_mix_logits = jnp.concatenate([grad_logit_first, grad_logit_second], axis=1)
        grad_mixing = jnp.dot(normed_two.T, grad_mix_logits, precision=highest)
        grad_constant = jnp.stack(
            [
                jnp.sum(mix_first[:, 1:2] * grad_first, axis=0),
                jnp.sum(mix_second[:, 1:2] * grad_second, axis=0),
            ],
            axis=0,
        )
        grad_normed_two = (
            grad_low_path
            + special_gates[:, 1:2] * grad_moe
            + mix_first[:, 0:1] * grad_first
            + mix_second[:, 0:1] * grad_second
            + jnp.dot(grad_mix_logits, held["mixing"].T, precision=highest)
        )
        grad_middle_norm, grad_moe_gain = rms_backward(
            held["middle"], held["inverse_two"], held["moe_gain"], grad_normed_two
        )
        grad_middle = grad_stream + grad_middle_norm
        grad_branch = grad_middle.astype(jnp.bfloat16)
        grad_output_w = jnp.einsum(
            "td,te->de", held["mixed_low"], grad_branch, preferred_element_type=jnp.float32
        )
        grad_mixed = (
            jnp.einsum(
                "te,de->td", grad_branch, weights["output"], preferred_element_type=jnp.float32
            )
            .astype(jnp.bfloat16)
            .reshape(count, heads, head_size)
        )
        grad_query_rot, grad_keys_rot, grad_values = attend_back(
            held["query_rot"],
            held["keys_rot"],
            held["values_low"],
            held["logsum"],
            grad_mixed,
            length,
            block,
        )
        grad_query = (
            rotate_back(grad_query_rot, cosine, sine).reshape(count, width).astype(jnp.bfloat16)
        )
        grad_keys = (
            rotate_back(grad_keys_rot, cosine, sine).reshape(count, width).astype(jnp.bfloat16)
        )
        grad_values_low = grad_values.reshape(count, width).astype(jnp.bfloat16)
        normed_low = held["normed_low"]
        grad_query_w = jnp.einsum(
            "td,te->de", normed_low, grad_query, preferred_element_type=jnp.float32
        )
        grad_key_w = jnp.einsum(
            "td,te->de", normed_low, grad_keys, preferred_element_type=jnp.float32
        )
        grad_value_w = jnp.einsum(
            "td,te->de", normed_low, grad_values_low, preferred_element_type=jnp.float32
        )
        grad_normed = jnp.einsum(
            "te,de->td", grad_query, weights["query"], preferred_element_type=jnp.float32
        )
        grad_normed = grad_normed + jnp.einsum(
            "te,de->td", grad_keys, weights["key"], preferred_element_type=jnp.float32
        )
        grad_normed = grad_normed + jnp.einsum(
            "te,de->td", grad_values_low, weights["value"], preferred_element_type=jnp.float32
        )
        grad_input_norm, grad_attn_gain = rms_backward(
            held["stream_in"], held["inverse"], held["attn_gain"], grad_normed
        )
        grad_stream = grad_middle + grad_input_norm
        layer_grads["query"] = grad_query_w
        layer_grads["key"] = grad_key_w
        layer_grads["value"] = grad_value_w
        layer_grads["output"] = grad_output_w
        layer_grads["router"] = grad_router
        layer_grads["mixing"] = grad_mixing
        layer_grads["constant"] = grad_constant
        layer_grads["attn_gain"] = grad_attn_gain
        layer_grads["moe_gain"] = grad_moe_gain
        dense_grads[depth] = layer_grads
        expert_grads[depth] = jnp.stack([grad_gate_w, grad_up_w, grad_down_w], axis=0)[None, None]
    expert_shard = lax.psum_scatter(
        jnp.concatenate(expert_grads, axis=1).astype(jnp.bfloat16),
        "dp",
        scatter_dimension=3,
        tiled=True,
    ).astype(jnp.float32)
    flat_grads = pack(dense_grads, width, routed, whole_size)
    within = lax.psum_scatter(
        flat_grads.reshape(lax.axis_size("dp"), groups, -1).astype(jnp.bfloat16),
        "group",
        scatter_dimension=1,
        tiled=True,
    )
    dense_shard = (
        lax.psum_scatter(within, "dp", scatter_dimension=0, tiled=True)
        .astype(jnp.float32)
        .reshape(-1)
    )
    gain_local = jnp.stack(
        [
            jnp.stack([dense_grads[depth]["attn_gain"], dense_grads[depth]["moe_gain"]], axis=0)
            for depth in range(LAYERS)
        ],
        axis=0,
    )
    local_square = jnp.sum(dense_shard * dense_shard) + jnp.sum(expert_shard * expert_shard)
    square_sum, gain_total = lax.psum((local_square, gain_local), ("dp", "group"))
    factor = jnp.minimum(1.0, clip_norm / (jnp.sqrt(square_sum) + 1e-06))
    dense_clip = dense_shard * factor
    expert_clip = expert_shard * factor
    dense_step = adam_delta(dense_master, dense_moment, dense_second, dense_clip)
    expert_step = adam_delta(expert_master, expert_moment, expert_second, expert_clip)
    return (
        output,
        grad_stream,
        dense_clip,
        expert_clip,
        gain_total * factor,
        dense_step,
        expert_step,
    )


def solution(mesh):
    return jax.shard_map(
        on_device,
        mesh=mesh,
        in_specs=(
            P(("dp", "group"), None),
            P(("dp", "group"), None),
            P(("dp", "group")),
            P(("dp", "group"), None),
            P(None, ("dp", "group"), None),
            P(("dp", "group")),
            P(("dp", "group")),
            P(("dp", "group")),
            P("group", None, None, "dp", None),
            P("group", None, None, "dp", None),
            P("group", None, None, "dp", None),
        ),
        out_specs=(
            P(("dp", "group"), None),
            P(("dp", "group"), None),
            P(("dp", "group")),
            P("group", None, None, "dp", None),
            P(),
            P(("dp", "group")),
            P("group", None, None, "dp", None),
        ),
        check_vma=False,
    )
```

profile of v0, /device:TPU:0, one launch (start us, length us, event | category | flops | bytes accessed | tf_op | source)
XLA Modules:
  0.0 1699.9 jit_solution(5782503753597767441)
XLA Ops:
  21.2 5.4 mul.1563
  31.2 65.0 %all-gather.3.cloned.1.call-done = bf16[4751360]{0:T(1024)(128)(2,1)} async-done(((bf16[148480]{0:T(1024)(128)(2,1)}), bf16[4751360]{0:T(1024)(128)(2,1)}) %all-gather.3.cloned.1.call-update) | async-done | bytes 9502736 | tf_op jit(solution)/shard_map/all_gather | solution.py:198
  96.2 6.5 fusion.172
  142.1 4.6 reshape.836
  146.7 6.2 scatter_custom_fusion
  161.9 6.5 gather_fusion.4
  193.7 265.1 %all-gather.5.cloned.1.call-done = bf16[1,2,3,2048,768]{4,3,2,1,0:T(8,128)(2,1)} async-done(((bf16[1,2,3,256,768]{4,3,2,1,0:T(8,128)(2,1)}), bf16[1,2,3,2048,768]{4,3,2,1,0:T(8,128)(2,1)}) %all-gather.5.cloned.1.call-update) | async-done | bytes 18874384 | tf_op jit(solution)/shard_map/all_gather | solution.py:202
  462.1 6.0 multiply_convert_fusion.9
  477.8 8.8 all-to-all-done.1
  486.8 5.2 gather_fusion
  492.0 4.9 reshape.874
  496.9 16.1 multiply_reduce_fusion.5
  537.9 6.5 gather_fusion.5
  547.1 4.9 reshape.844
  552.0 5.8 scatter_custom_fusion.1
  564.3 6.4 scatter_custom_fusion.2
  579.6 5.1 fusion.37
  584.7 4.8 fusion.35
  589.7 6.7 multiply_convert_fusion.6
  613.1 4.9 all-to-all-done.5
  625.6 5.2 gather_fusion.2
  630.8 4.9 reshape.876
  635.7 6.8 reduce_sum.615
  644.5 5.3 gather_fusion.1
  649.8 5.0 reshape.875
  654.8 18.3 %multiply_reduce_fusion.3 = (f32[512,2]{1,0:T(8,128)}, f32[512,768]{1,0:T(8,128)S(1)}) fusion(f32[512,2,768]{2,1,0:T(2,128)} %reshape.875, f32[512,768]{1,0:T(8,128)S(1)} %copy-done.16, f32[512,2]{1,0:T(8,128)} %copy-done.58), kind=kLoop, calls=%fused_computation.69 | loop fusion | flops 2751488 | bytes 6299648 | tf_op jit(solution)/shard_map/reduce_sum | solution.py:382
  687.7 11.5 multiply_reduce_fusion.1
  700.6 7.1 multiply_convert_fusion.1
  738.7 5.4 mul.1629
  744.1 6.4 scatter_custom_fusion.3
  778.1 5.8 multiply_convert_fusion.4
  799.8 6.1 all-to-all-done.7
  806.1 5.3 gather_fusion.3
  811.3 4.9 reshape.877
  816.2 6.9 reduce_sum.632
  830.9 11.0 multiply_reduce_fusion
  842.2 7.2 multiply_convert_fusion
  889.8 146.8 %concatenate.80 = bf16[4751360]{0:T(1024)(128)(2,1)} concatenate(bf16[589824]{0:T(1024)(128)(2,1)} %reshape.772, bf16[589824]{0:T(1024)(128)(2,1)} %reshape.773, bf16[589824]{0:T(1024)(128)(2,1)} %reshape.774, bf16[589824]{0:T(1024)(128)(2,1)} %reshape.775, bf16[6144]{0:T(1024)(128)(2,1)} %reshape.776, bf16[3072]{0:T(1024)(128)(2,1)} %reshape.777, bf16[1536]{0:T(1024)(128)(2,1)} %reshape.778, ...), dimensions={0} | concatenate | bytes 19005440 | tf_op jit(solution)/shard_map/concatenate | solution.py:57
  1036.6 10.9 convert_element_type.347
  1047.5 11.7 copy.203
  1067.4 5.7 maximum_bitcast_fusion.1
  1073.2 64.2 %reduce-scatter.3.cloned.1.call-done = bf16[8,1,148480]{2,0,1:T(8,128)(2,1)} async-done(((bf16[8,4,148480]{2,0,1:T(8,128)(2,1)}), bf16[8,1,148480]{2,0,1:T(8,128)(2,1)}) %reduce-scatter.3.cloned.1.call-update) | async-done | bytes 2375696 | tf_op jit(solution)/shard_map/reduce_scatter | solution.py:522
  1137.3 5.6 copy.204
  1153.7 8.1 pad_maximum_fusion
  1163.1 151.0 %all-reduce.8.cloned.1.call-done = bf16[8,1,148480]{2,1,0:T(2,128)(2,1)} async-done(((bf16[8,1,148480]{2,1,0:T(2,128)(2,1)}), bf16[8,1,148480]{2,1,0:T(2,128)(2,1)}) %all-reduce.8.cloned.1.call-update) | async-done | bytes 2375696
  1317.6 313.2 %reduce-scatter.5.cloned.1.call-done = bf16[1,2,3,256,768]{4,3,2,1,0:T(8,128)(2,1)} async-done(((bf16[1,2,3,2048,768]{4,3,2,1,0:T(8,128)(2,1)}), bf16[1,2,3,256,768]{4,3,2,1,0:T(8,128)(2,1)}) %reduce-scatter.5.cloned.1.call-update) | async-done | bytes 2359312 | tf_op jit(solution)/shard_map/reduce_scatter | solution.py:515
  1638.6 39.5 %all-reduce.5 = (f32[]{:T(128)}, f32[2,2,768]{2,1,0:T(2,128)S(1)}) all-reduce(f32[]{:T(128)S(6)} %add.431, f32[2,2,768]{2,1,0:T(2,128)S(1)} %pad_maximum_fusion.13), channel_id=1, replica_groups=mesh['dp'=8,'group'=4] {'dp','group'}, use_global_device_ids=true, to_apply=%region_81.83 | all-reduce | flops 3073 | bytes 24584 | tf_op jit(solution)/shard_map/psum | solution.py:541
  1683.9 9.0 fusion.19
  (779 shorter events, 345.5 us)
Async XLA Ops:
  7.2 89.0 %all-gather.3.cloned.1.call-start = ((), (), s32[]{:S(2)}) async-start(), calls=%async_computation.10 | async-start | bytes 9799680 | tf_op jit(solution)/shard_map/all_gather | solution.py:198
  9.0 449.8 %all-gather.5.cloned.1.call-start = ((), (), s32[]{:S(2)}) async-start(), calls=%async_computation.11 | async-start | bytes 21233664 | tf_op jit(solution)/shard_map/all_gather | solution.py:202
  28.9 97.3 %copy-start.184 = (f32[512]{0:T(512)}, f32[512]{0:T(512)S(1)}, u32[]{:S(2)}) copy-start(f32[512]{0:T(512)S(1)} %get-tuple-element.142) | copy-start | bytes 6148
  29.0 457.8 %copy-start.6 = (s32[1024]{0:T(1024)}, s32[1024]{0:T(1024)S(1)}, u32[]{:S(2)}) copy-start(s32[1024]{0:T(1024)S(1)} %broadcast_clamp_fusion.1) | copy-start | bytes 12292
  31.1 490.8 %copy-start.64 = (f32[512,32]{0,1:T(8,128)}, f32[512,32]{0,1:T(8,128)S(1)}, u32[]{:S(2)}) copy-start(f32[512,32]{0,1:T(8,128)S(1)} %get-tuple-element.149) | copy-start | bytes 196612
  31.1 490.8 %copy-start.66 = (f32[512,32]{0,1:T(8,128)}, f32[512,32]{0,1:T(8,128)S(1)}, u32[]{:S(2)}) copy-start(f32[512,32]{0,1:T(8,128)S(1)} %get-tuple-element.150) | copy-start | bytes 196612
  139.2 373.8 %copy-start.4 = (f32[512,768]{1,0:T(8,128)}, f32[512,768]{1,0:T(8,128)S(1)}, u32[]{:S(2)}) copy-start(f32[512,768]{1,0:T(8,128)S(1)} %get-tuple-element.154) | copy-start | bytes 4718596
  139.9 373.1 %copy-start.127 = (f32[512]{0:T(512)}, f32[512]{0:T(512)S(1)}, u32[]{:S(2)}) copy-start(f32[512]{0:T(512)S(1)} %get-tuple-element.144) | copy-start | bytes 6148
  140.1 20.8 %copy-start.22 = (bf16[512,768]{1,0:T(8,128)(2,1)}, bf16[512,768]{1,0:T(8,128)(2,1)S(1)}, u32[]{:S(2)}) copy-start(bf16[512,768]{1,0:T(8,128)(2,1)S(1)} %fusion.79) | copy-start | bytes 2359300
  155.8 36.7 %all-to-all-start = ((bf16[4,90,768]{2,1,0:T(8,128)(2,1)}), bf16[4,90,768]{2,1,0:T(8,128)(2,1)}, u32[]{:S(2)}, u32[]{:S(2)}) async-start(bf16[4,90,768]{2,1,0:T(8,128)(2,1)} %reshape.748), calls=%async_computation | async-start | bytes 1179648 | tf_op jit(solution)/shard_map/all_to_all | solution.py:242
  161.9 375.8 %copy-start = (f32[512,8]{0,1:T(8,128)}, f32[512,8]{0,1:T(8,128)S(1)}, u32[]{:S(2)}) copy-start(f32[512,8]{0,1:T(8,128)S(1)} %fusion.181) | copy-start | bytes 49156
  191.8 270.3 %copy-start.140 = (f32[512,2]{0,1:T(2,128)}, f32[512,2]{0,1:T(2,128)S(1)}, u32[]{:S(2)}) copy-start(f32[512,2]{0,1:T(2,128)S(1)} %get-tuple-element.130) | copy-start | bytes 12292
  191.8 270.3 %copy-start.142 = (f32[512,2]{0,1:T(2,128)}, f32[512,2]{0,1:T(2,128)S(1)}, u32[]{:S(2)}) copy-start(f32[512,2]{0,1:T(2,128)S(1)} %get-tuple-element.129) | copy-start | bytes 12292
  191.8 321.2 %copy-start.176 = (f32[512,1]{0,1:T(1,128)}, f32[512,1]{0,1:T(1,128)S(1)}, u32[]{:S(2)}) copy-start(f32[512,1]{0,1:T(1,128)S(1)} %get-tuple-element.137) | copy-start | bytes 6148
  191.8 321.2 %copy-start.178 = (f32[512,1]{0,1:T(1,128)}, f32[512,1]{0,1:T(1,128)S(1)}, u32[]{:S(2)}) copy-start(f32[512,1]{0,1:T(1,128)S(1)} %get-tuple-element.172) | copy-start | bytes 6148
  191.9 321.2 %copy-start.187 = (f32[512,1]{0,1:T(1,128)}, f32[512,1]{0,1:T(1,128)S(1)}, u32[]{:S(2)}) copy-start(f32[512,1]{0,1:T(1,128)S(1)} %get-tuple-element.138) | copy-start | bytes 6148
  191.9 321.2 %copy-start.189 = (f32[512,1]{0,1:T(1,128)}, f32[512,1]{0,1:T(1,128)S(1)}, u32[]{:S(2)}) copy-start(f32[512,1]{0,1:T(1,128)S(1)} %get-tuple-element.171) | copy-start | bytes 6148
  192.5 320.6 %copy-start.162 = (f32[768]{0:T(1024)}, f32[768]{0:T(1024)S(1)}, u32[]{:S(2)}) copy-start(f32[768]{0:T(1024)S(1)} %get-tuple-element.169) | copy-start | bytes 9220
  192.5 320.6 %copy-start.164 = (f32[768]{0:T(1024)}, f32[768]{0:T(1024)S(1)}, u32[]{:S(2)}) copy-start(f32[768]{0:T(1024)S(1)} %get-tuple-element.170) | copy-start | bytes 9220
  193.7 268.4 %copy-start.101 = (bf16[360,768]{1,0:T(8,128)(2,1)}, bf16[360,768]{1,0:T(8,128)(2,1)S(1)}, u32[]{:S(2)}) copy-start(bf16[360,768]{1,0:T(8,128)(2,1)S(1)} %reshape.749) | copy-start | bytes 1658884
  473.4 13.2 all-to-all-start.1
  477.1 36.0 %copy-start.172 = (f32[512,1]{0,1:T(1,128)}, f32[512,1]{0,1:T(1,128)S(1)}, u32[]{:S(2)}) copy-start(f32[512,1]{0,1:T(1,128)S(1)} %get-tuple-element.127) | copy-start | bytes 6148
  477.1 36.0 %copy-start.174 = (f32[512,1]{0,1:T(1,128)}, f32[512,1]{0,1:T(1,128)S(1)}, u32[]{:S(2)}) copy-start(f32[512,1]{0,1:T(1,128)S(1)} %get-tuple-element.128) | copy-start | bytes 6148
  477.1 36.0 %copy-start.183 = (f32[512,1]{0,1:T(1,128)}, f32[512,1]{0,1:T(1,128)S(1)}, u32[]{:S(2)}) copy-start(f32[512,1]{0,1:T(1,128)S(1)} %get-tuple-element.126) | copy-start | bytes 6148
  536.4 146.5 %copy-start.133 = (f32[512]{0:T(512)}, f32[512]{0:T(512)S(1)}, u32[]{:S(2)}) copy-start(f32[512]{0:T(512)S(1)} %get-tuple-element.148) | copy-start | bytes 6148
  545.0 19.1 %copy-start.58 = (f32[512,2]{1,0:T(8,128)}, f32[512,2]{1,0:T(8,128)S(1)}, u32[]{:S(2)}) copy-start(f32[512,2]{1,0:T(8,128)S(1)} %copy.182) | copy-start | bytes 12292
  560.6 14.1 all-to-all-start.2
  574.7 14.9 all-to-all-start.4
  605.0 13.0 all-to-all-start.5
  613.1 12.5 copy-start.8
  618.8 23.7 %all-to-all-start.3 = ((bf16[4,90,768]{2,1,0:T(8,128)(2,1)}), bf16[4,90,768]{2,1,0:T(8,128)(2,1)S(1)}, u32[]{:S(2)}, u32[]{:S(2)}) async-start(bf16[4,90,768]{2,1,0:T(8,128)(2,1)} %reshape.760), calls=%async_computation.3 | async-start | bytes 1179648 | tf_op jit(solution)/shard_map/all_to_all | solution.py:258
  654.7 18.3 %copy-start.196 = (f32[768]{0:T(1024)S(1)}, f32[768]{0:T(1024)}, u32[]{:S(2)}) copy-start(f32[768]{0:T(1024)} %get-tuple-element.116) | copy-start | bytes 9220
  654.7 18.3 %copy-start.197 = (f32[768]{0:T(1024)S(1)}, f32[768]{0:T(1024)}, u32[]{:S(2)}) copy-start(f32[768]{0:T(1024)} %get-tuple-element.117) | copy-start | bytes 9220
  687.7 12.9 slice-start.5
  714.6 13.4 copy-start.95
  751.7 25.1 %all-to-all-start.6 = ((bf16[4,90,768]{2,1,0:T(8,128)(2,1)}), bf16[4,90,768]{2,1,0:T(8,128)(2,1)}, u32[]{:S(2)}, u32[]{:S(2)}) async-start(bf16[4,90,768]{2,1,0:T(8,128)(2,1)} %reshape.767), calls=%async_computation.6 | async-start | bytes 1179648 | tf_op jit(solution)/shard_map/all_to_all | solution.py:338
  792.5 13.4 all-to-all-start.7
  796.4 341.0 %reduce-scatter.3.cloned.1.call-start = ((), (), s32[]{:S(2)}) async-start(), calls=%async_computation.12 | async-start | bytes 11878400 | tf_op jit(solution)/shard_map/reduce_scatter | solution.py:522
  830.1 11.8 copy-start.49
  830.1 11.8 slice-start
  1059.2 254.9 %all-reduce.8.cloned.1.call-start = ((), (), s32[]{:S(2)}) async-start(), calls=%async_computation.14 | async-start | bytes 9502720
  1143.0 487.8 %reduce-scatter.5.cloned.1.call-start = ((), (), s32[]{:S(2)}) async-start(), calls=%async_computation.13 | async-start | bytes 21233664 | tf_op jit(solution)/shard_map/reduce_scatter | solution.py:515
  1161.8 473.7 %copy-start.161 = (f32[768]{0:T(1024)S(1)}, f32[768]{0:T(1024)}, u32[]{:S(2)}) copy-start(f32[768]{0:T(1024)} %copy-done.159) | copy-start | bytes 9220
  1161.8 473.7 %copy-start.186 = (f32[512]{0:T(512)S(1)}, f32[512]{0:T(512)}, u32[]{:S(2)}) copy-start(f32[512]{0:T(512)} %copy-done.184) | copy-start | bytes 6148
  1161.8 473.7 %copy-start.198 = (f32[512]{0:T(512)S(1)}, f32[512]{0:T(512)}, u32[]{:S(2)}) copy-start(f32[512]{0:T(512)} %get-tuple-element.141) | copy-start | bytes 6148
  1635.6 46.2 %copy-start.100 = (f32[148480]{0:T(1024)S(1)}, f32[148480]{0:T(1024)}, u32[]{:S(2)}) copy-start(f32[148480]{0:T(1024)} %param.19) | copy-start | bytes 1781764
  1638.6 43.2 %copy-start.55 = (f32[148480]{0:T(1024)S(1)}, f32[148480]{0:T(1024)}, u32[]{:S(2)}) copy-start(f32[148480]{0:T(1024)} %param.18) | copy-start | bytes 1781764
  1638.6 43.2 %copy-start.99 = (f32[148480]{0:T(1024)S(1)}, f32[148480]{0:T(1024)}, u32[]{:S(2)}) copy-start(f32[148480]{0:T(1024)} %param.20) | copy-start | bytes 1781764
  (202 other events, 767.0 us)
Sparse Core Ops, SparseCore 0:
  11.4 84.7 all-gather.2
  97.7 361.0 all-gather.4
  1059.3 77.9 reduce-scatter.2
  1143.1 171.0 all-reduce.7
  1317.9 312.8 reduce-scatter.4
where the time goes:
time: 1730 us; the launch traced here: 1700 us
  waiting for transfers between devices  878 us (51%)
  local copies, waits for them, and re-layouts  400 us (23%)
  matrix products  179 us (10%)
  other arithmetic  152 us (9%)
  blocking collectives  39.5 us (2%)
  starting transfers between devices  30.9 us (2%)
  between operations  20.3 us (1%)
    reduce_scatter x1, waiting for transfers between devices, on_device(): lax.psum_scatter(jnp.concatenate(expert_grads, axis=1).astype(jnp.bfloat1...  313 us
    all_gather x1, waiting for transfers between devices, on_device(): lax.all_gather(expert_master.astype(jnp.bfloat16), 'dp', axis=3, tiled=True)  265 us
    unnamed x6, waiting for transfers between devices  151 us
    concatenate x1, local copies, waits for them, and re-layouts, pack(): jnp.concatenate([flat, jnp.zeros((whole_size - flat.shape[0],), jnp.float...  147 us
    all_gather x1, waiting for transfers between devices, on_device(): lax.all_gather(dense_master.astype(jnp.bfloat16), ('dp', 'group'), axis=0...  65 us
    reduce_scatter x1, waiting for transfers between devices, on_device(): lax.psum_scatter(flat_grads.reshape(lax.axis_size('dp'), groups, -1).asty...  64.2 us
    psum x1, blocking collectives, on_device(): lax.psum((local_square, gain_local), ('dp', 'group'))  39.5 us
  transfers between devices with their start and end apart: 13, of which 8 were waited for; matrix products, arithmetic and copies ran while one was open for 13% of the time, Pallas kernels for 0%

commit v1 on v0

v1 whole, which is shorter than its diff:
```python
import functools

import jax
import numpy as np
import jax.numpy as jnp
from jax import lax
from jax.experimental import pallas as pl
from jax.experimental.pallas import tpu as pltpu
from jax.sharding import PartitionSpec as P

HEADS = 12
LAYERS = 2


norm_eps = 1e-06
rope_base = 10000.0
neg_big = -1e30
adam_rate = 0.001
beta_one = 0.9
beta_two = 0.95
adam_eps = 1e-08
decay_rate = 0.1
clip_norm = 1.0
step_number = 10
highest = lax.Precision.HIGHEST
f32 = jnp.float32
bf16 = jnp.bfloat16
ALL = ("dp", "group")


def layout(width, routed):
    items = []
    for depth in range(LAYERS):
        items = items + [
            (depth, "query", (width, width)),
            (depth, "key", (width, width)),
            (depth, "value", (width, width)),
            (depth, "output", (width, width)),
            (depth, "router", (width, routed)),
            (depth, "mixing", (width, 4)),
            (depth, "constant", (2, width)),
            (depth, "attn_gain", (width,)),
            (depth, "moe_gain", (width,)),
        ]
        if depth > 0:
            items.append((depth, "carry", (routed, routed)))
    return items


def unpack(flat, width, routed):
    params = [dict() for depth in range(LAYERS)]
    cursor = 0
    for depth, name, shape in layout(width, routed):
        amount = 1
        for extent in shape:
            amount = amount * extent
        params[depth][name] = flat[cursor : cursor + amount].reshape(shape)
        cursor = cursor + amount
    return params


class Wires:
    def __init__(self):
        self.groups = lax.axis_size("group")
        self.dp = lax.axis_size("dp")
        self.tops = self.dp // 4
        self.me_dp = lax.axis_index("dp")
        self.me_group = lax.axis_index("group")

    def swap(self, array, h=0, l=0, x=0, g=0):
        off = h * 4 + l * 2 + x
        pairs = [
            (d * self.groups + k, (d ^ off) * self.groups + (k ^ g))
            for d in range(self.dp)
            for k in range(self.groups)
        ]
        return lax.ppermute(array, ALL, pairs)


def pin(values, *after):
    return lax.optimization_barrier((values, after))[0]


def axis_step(axis):
    return dict(l=dict(l=1), x=dict(x=1), y=dict(g=2), c=dict(g=1))[axis]


AXIS_VALUE = dict(l=8, x=4, y=2, c=1)


def plan_thirds(tiles):
    step = tiles // 3
    first = tiles - 2 * step
    return (
        (("l", "x", "y"), 0, first),
        (("x", "y", "l"), first, step),
        (("y", "l", "x"), first + step, step),
    )


def plan_halves(tiles):
    half = tiles // 2
    return ((("l", "x", "y"), 0, tiles - half), (("l", "y", "x"), tiles - half, half))


def grow(wires, parts, plan, step):
    return [
        jnp.concatenate([v, wires.swap(v, **axis_step(axes[step]))], axis=0)
        for v, (axes, _, _) in zip(parts, plan)
    ]


class ScatterDense:
    def __init__(self, wires, halves, plan):
        self.wires = wires
        self.halves = halves
        self.plan = plan

    def send(self, step, *after):
        self.got = []
        for (_, give), (axes, _, _) in zip(self.halves, self.plan):
            axis = (("c",) + axes[::-1])[step]
            give = pin(give, *after) if after else give
            self.got.append(self.wires.swap(give, **axis_step(axis)))

    def add(self):
        halves = []
        for (keep, _), got in zip(self.halves, self.got):
            if keep.shape[0] == 1:
                halves.append(((keep[0].astype(f32) + got[0].astype(f32)).astype(bf16), None))
                continue
            half = keep.shape[0] // 2
            cut = lambda a, b: (keep[a:b].astype(f32) + got[a:b].astype(f32)).astype(bf16)
            halves.append((cut(0, half), cut(half, 2 * half)))
        self.halves = halves

    def done(self):
        return jnp.concatenate([keep for keep, _ in self.halves], axis=0)


def cut_far(part):
    half = part.shape[1] // 2
    return [part[:, :half], part[:, half:]]


class ScatterExpert:
    def __init__(self, wires, parts):
        self.wires = wires
        self.near = parts[:2]
        self.far = parts[2:]

    def first(self):
        self.got = [self.wires.swap(v, x=1) for v in self.far[1::2]]

    def second(self, *after):
        sums = [
            (pin(a, *after).astype(f32) + b.astype(f32)).astype(bf16)
            for a, b in zip(self.far[0::2], self.got)
        ]
        self.got_far = [self.wires.swap(v, h=1 + i // 2) for i, v in enumerate(sums)]
        self.got_near = self.wires.swap(pin(self.near[1], *sums), x=1)

    def received(self):
        return [*self.got_far, self.got_near]

    def done(self):
        total = self.near[0].astype(f32) + self.got_near.astype(f32)
        for i in range(0, len(self.got_far), 2):
            total = total + jnp.concatenate(self.got_far[i : i + 2], axis=1).astype(f32)
        return total


def exchange_out(wires, pairs, after=()):
    half = len(pairs)
    got = [pairs[0]]
    for l in range(2):
        for y in range(half):
            if l or y:
                got.append(wires.swap(pairs[y], l=l, g=2 * y))
    room = pairs[0].shape[0] // 2
    crossed = wires.swap(jnp.concatenate([v[room:] for v in got], axis=0), g=1)
    return [*got, crossed]


def exchange_back(wires, near, crossed):
    count = 2 * (wires.groups // 2)
    room = near.shape[0] // count
    other = wires.swap(crossed, g=1)
    got = []
    for i in range(count):
        l, y = divmod(i, wires.groups // 2)
        s = slice(i * room, (i + 1) * room)
        pair = jnp.concatenate([near[s], other[s]], axis=0)
        got.append(pair if i == 0 else wires.swap(pair, l=l, g=2 * y))
    return got


def adam_delta(master, moment, second, grad):
    moment_new = beta_one * moment + (1.0 - beta_one) * grad
    second_new = beta_two * second + (1.0 - beta_two) * grad * grad
    fix_one = 1.0 - beta_one**step_number
    fix_two = 1.0 - beta_two**step_number
    direction = moment_new / fix_one / (jnp.sqrt(second_new / fix_two) + adam_eps)
    return adam_rate * (direction + decay_rate * master)


VM = pl.BlockSpec(memory_space=pltpu.VMEM)
SM = pl.BlockSpec(memory_space=pltpu.SMEM)
ANY = pl.BlockSpec(memory_space=pl.ANY)
LANES = 128
MIX = 32
SLOT = 48
INV = 50
PARAMS = dict(vmem_limit_bytes=60 * 1024 * 1024)


def dot(a, b):
    return lax.dot_general(a, b, (((1,), (0,)), ((), ())), preferred_element_type=f32)


def dot_nt(a, b):
    return lax.dot_general(a, b, (((1,), (1,)), ((), ())), preferred_element_type=f32)


def dot_tn(a, b):
    return lax.dot_general(a, b, (((0,), (0,)), ((), ())), preferred_element_type=f32)


def split(v):
    high = v.astype(bf16)
    return high, (v - high.astype(f32)).astype(bf16)


def lane_of(rows):
    return lax.broadcasted_iota(jnp.int32, (rows, LANES), 1)


def take_lane(v, lane, at):
    return jnp.sum(jnp.where(lane == at, v, 0.0), axis=1, keepdims=True)


def put_lanes(lane, pairs):
    out = jnp.zeros(lane.shape, f32)
    for at, column in pairs:
        out = jnp.where(lane == at, column, out)
    return out


def blocks(count, size, body):
    def step(i, none):
        body(pl.multiple_of(i * size, size))
        return none

    lax.fori_loop(0, count // size, step, 0)


def half_mask(hd):
    lane = lane_of(1)
    mine = lane < 64 if hd == 0 else lane >= 64
    return jnp.where(mine, 1.0, 0.0).astype(bf16)


def rope_turn(v, cos, sin, lane):
    other = jnp.where(lane % 64 < 32, pltpu.roll(v, 96, 1), pltpu.roll(v, 32, 1))
    return v * cos + other * sin


def two_softmax(a, b):
    top = jnp.maximum(a, b)
    ea, eb = jnp.exp(a - top), jnp.exp(b - top)
    total = ea + eb
    return ea / total, eb / total


class Columns:
    def __init__(self, side, routes, groups):
        lane = lane_of(side.shape[0])
        self.lane = lane
        self.routes = [routes[:, k : k + 1] for k in range(2)]
        self.hot = [lane == r for r in self.routes]
        chosen = [jnp.sum(jnp.where(h, side, 0.0), axis=1, keepdims=True) for h in self.hot]
        self.gates = two_softmax(*chosen)
        mixes = [take_lane(side, lane, MIX + j) for j in range(4)]
        self.first = two_softmax(mixes[0], mixes[1])
        self.second = two_softmax(mixes[2], mixes[3])
        self.special = [
            sum(jnp.where(self.routes[k] == groups + j, self.gates[k], 0.0) for k in range(2))
            for j in range(4)
        ]
        self.normed_part = (
            self.special[1]
            + self.special[2] * self.first[0]
            + self.special[3] * self.second[0]
        )
        self.constant_part = (self.special[2] * self.first[1], self.special[3] * self.second[1])
        self.slots = [take_lane(side, lane, SLOT + k) for k in range(2)]
        self.inverse = take_lane(side, lane, INV)
        self.inverse_two = take_lane(side, lane, INV + 1)


def add_tables(back, table, room):
    half = len(back) // 2
    for y in range(half):

        def add(r, y=y):
            s = pl.ds(r, 16)
            total = back[y][s, :].astype(f32) + back[half + y][s, :].astype(f32)
            table[pl.ds(2 * y * room + r, 16), :] = total.astype(bf16)

        blocks(2 * room, 16, add)


def combine_body(cols, mid, ret, vecs, table, hots, out, room):
    count, width = mid.shape
    rows = table.shape[0]
    add_tables(ret, table, room)
    at = lax.broadcasted_iota(jnp.int32, (count, rows), 1).astype(f32)
    for k in range(2):
        hots[k][...] = jnp.where(at == cols.slots[k], 1.0, 0.0).astype(bf16)

    def piece(c):
        s = pl.ds(c, LANES)
        m = mid[:, s]
        normed = m * cols.inverse_two * vecs[3:4, s]
        y = m + cols.gates[0] * dot(hots[0][...], table[:, s])
        y = y + cols.gates[1] * dot(hots[1][...], table[:, s])
        y = y + cols.normed_part * normed
        y = y + cols.constant_part[0] * vecs[0:1, s] + cols.constant_part[1] * vecs[1:2, s]
        out[:, s] = y.astype(out.dtype)

    blocks(width, LANES, piece)


def visible_bias(bias, length, flip):
    count = bias.shape[0]

    def piece(r):
        shape = (32, count)
        a = lax.broadcasted_iota(jnp.int32, shape, 0) + r
        b = lax.broadcasted_iota(jnp.int32, shape, 1)
        key, query = (a, b) if flip else (b, a)
        bias[pl.ds(r, 32), :] = jnp.where((key <= query) & (key < length), 0.0, neg_big)

    blocks(count, 32, piece)


def forward_kernel(static, *refs):
    depth, groups, capacity, room, eps, n_after = static
    refs = list(refs)
    take = lambda n: [refs.pop(0) for _ in range(n)]
    ints, order_row, order_col, routes, w_hbm, wsm, vecs, cos, sin = take(9)
    if depth == 0:
        (source,) = take(1)
    else:
        side_in, routes_in, mid_in, vecs_in, wg, cot = take(6)
        ret = take(groups)
    take(n_after)
    send = take(groups // 2)
    if depth > 0:
        send_grads = take(groups // 2)
    n1, q_out, k_out, v_out, mixed, lse_out, middle, side_out = take(8)
    if depth > 0:
        (stream,) = take(1)
    w, bias, n2h, n2l, lse, sems = take(6)
    if depth > 0:
        table, hot0, hot1 = take(3)
    count, width = n1.shape
    routed = groups + 4
    length, me = ints[0], ints[1]
    loads = [pltpu.make_async_copy(w_hbm.at[i], w.at[i], sems.at[i]) for i in range(4)]
    for c in loads:
        c.start()
    visible_bias(bias, length, False)
    lane = lane_of(count)

    if depth > 0:
        before = Columns(side_in[...], routes_in[...], groups)
        combine_body(before, mid_in, ret, vecs_in, table, (hot0, hot1), stream, room)
        source = stream

    def norm_one(r):
        s = pl.ds(r, 64)
        x = source[s, :].astype(f32)
        inverse = lax.rsqrt(jnp.mean(x * x, axis=1, keepdims=True) + eps)
        n1[s, :] = (x * inverse * vecs[2:3, :]).astype(bf16)
        side_out[s, :] = jnp.where(lane_of(64) == INV, inverse, 0.0)

    blocks(count, 64, norm_one)

    for kind in range(3):
        loads[kind].wait()

        def project(c, kind=kind):
            s = pl.ds(c, 256)
            y = dot(n1[...], w[kind, :, s])
            for half in range(2):
                part = y[:, half * LANES : (half + 1) * LANES]
                t = pl.ds(pl.multiple_of(c + half * LANES, LANES), LANES)
                if kind == 2:
                    v_out[:, t] = part.astype(bf16)
                else:
                    part = rope_turn(part, cos[...], sin[...], lane)
                    if kind == 0:
                        q_out[:, t] = (part * 0.125).astype(bf16)
                    else:
                        k_out[:, t] = part.astype(bf16)

        blocks(width, 256, project)

    half_rows = count // 2

    def attend_pair(c):
        t = pl.ds(c, LANES)
        pair = c // LANES
        for qb in range(2):
            rows = pl.ds(qb * half_rows, half_rows)
            span = (qb + 1) * half_rows
            q2 = q_out[rows, t]
            k2 = k_out[0:span, t]
            v2 = v_out[0:span, t]
            low_half = lane_of(half_rows) < 64
            outs = []
            for hd in range(2):
                qm = q2 * half_mask(hd)
                s = dot_nt(qm, k2) + bias[rows, 0:span]
                peak = jnp.max(s, axis=1, keepdims=True)
                e = jnp.exp(s - peak)
                total = jnp.sum(e, axis=1, keepdims=True)
                outs.append(dot(e.astype(bf16), v2) * (1.0 / total))
                lse[rows, :] = jnp.where(
                    lane_of(half_rows) == 2 * pair + hd, peak + jnp.log(total), lse[rows, :]
                )
            mixed[rows, t] = jnp.where(low_half, outs[0], outs[1]).astype(bf16)

    lse[...] = jnp.zeros(lse.shape, f32)
    blocks(width, LANES, attend_pair)
    lse_out[...] = jnp.transpose(lse[...])[0:16, :]
    loads[3].wait()

    def mix_out(c):
        s = pl.ds(c, 256)
        middle[:, s] = source[:, s].astype(f32) + dot(mixed[...], w[3, :, s])

    blocks(width, 256, mix_out)

    def norm_two(r):
        s = pl.ds(r, 64)
        x = middle[s, :]
        inverse = lax.rsqrt(jnp.mean(x * x, axis=1, keepdims=True) + eps)
        high, rest = split(x * inverse * vecs[3:4, :])
        n2h[s, :] = high
        n2l[s, :] = rest
        side_out[s, :] = side_out[s, :] + jnp.where(lane_of(64) == INV + 1, inverse, 0.0)

    blocks(count, 64, norm_two)
    both = dot(n2h[...], wsm[...])
    rest = dot(n2l[...], wsm[...])
    logits = jnp.where(lane < routed, both, 0.0)
    if depth > 0:
        held = jnp.where(lane < routed, side_in[...], 0.0)
        h1, h2 = split(held)
        h3 = (held - h1.astype(f32) - h2.astype(f32)).astype(bf16)
        logits = logits + dot(h1, wg[...]) + dot(h2, wg[...]) + dot(h3, wg[...])
    mixes = jnp.where((lane >= MIX) & (lane < MIX + 4), both + rest, 0.0)
    r = [routes[:, k : k + 1] for k in range(2)]
    token = lax.broadcasted_iota(jnp.int32, (count, 1), 0)
    live = token < length
    other = lax.broadcasted_iota(jnp.int32, (count, count), 1)
    earlier = jnp.where((order_row[...] < order_col[...]) & (other < length), 1.0, 0.0).astype(bf16)
    marks = jnp.where((lane == r[0]) | (lane == r[1]), 1.0, 0.0).astype(bf16)
    ranks = dot(earlier, marks)
    slots = []
    for k in range(2):
        rank = take_lane(ranks, lane, r[k])
        kept = (r[k] < groups) & live & (rank < capacity)
        slots.append(jnp.where(kept, ((r[k] ^ me) * room).astype(f32) + rank, -1.0))
    side = side_out[...] + logits + mixes
    side = side + jnp.where(lane == SLOT, slots[0], 0.0) + jnp.where(lane == SLOT + 1, slots[1], 0.0)
    side_out[...] = side
    turned = jnp.transpose(side)
    rows = groups * room
    at = lax.broadcasted_iota(jnp.int32, (rows, count), 0).astype(f32)
    is0 = at == turned[SLOT : SLOT + 1, :]
    is1 = at == turned[SLOT + 1 : SLOT + 2, :]
    place = jnp.where(is0 | is1, 1.0, 0.0).astype(bf16)

    def put(c):
        s = pl.ds(c, 256)
        put_blocks(send, dot(place, n2h[:, s]).astype(bf16), s, room)

    blocks(width, 256, put)
    if depth > 0:
        now = Columns(side, routes[...], groups)
        put_grads(now.gates, is0, is1, cot, send_grads, room)


def put_blocks(send, y, s, room):
    for i in range(len(send)):
        send[i][:, s] = y[2 * i * room : 2 * (i + 1) * room]


def put_grads(gates, is0, is1, grads, send, room):
    p0 = jnp.where(is0, 1.0, 0.0).astype(bf16)
    p1 = jnp.where(is1, 1.0, 0.0).astype(bf16)

    def put(c):
        s = pl.ds(c, LANES)
        g = grads[:, s]
        y = dot(p0, (gates[0] * g).astype(bf16)) + dot(p1, (gates[1] * g).astype(bf16))
        put_blocks(send, y.astype(bf16), s, room)

    blocks(grads.shape[1], LANES, put)


def layer_forward(depth, sizes, ints, order, routes, weights, source, tables, after=()):
    groups, capacity, room = sizes
    count, width = routes.shape[0], weights["w"].shape[1]
    sds = jax.ShapeDtypeStruct
    low = sds((count, width), bf16)
    pair = sds((2 * room, width), bf16)
    outs = [pair] * (groups // 2 * (depth + 1)) + [
        low,
        low,
        low,
        low,
        low,
        sds((16, count), f32),
        sds((count, width), f32),
        sds((count, LANES), f32),
    ]
    scratch = [
        pltpu.VMEM((4, width, width), bf16),
        pltpu.VMEM((count, count), f32),
        pltpu.VMEM((count, width), bf16),
        pltpu.VMEM((count, width), bf16),
        pltpu.VMEM((count, LANES), f32),
        pltpu.SemaphoreType.DMA((4,)),
    ]
    args = [
        ints,
        order.reshape(1, count),
        order.reshape(count, 1),
        routes,
        weights["w"],
        weights["small"],
        weights["vecs"],
        *tables,
    ]
    specs = [SM, VM, VM, VM, ANY, VM, VM, VM, VM]
    if depth > 0:
        outs += [sds((count, width), f32)]
        scratch += [
            pltpu.VMEM((groups * room, width), bf16),
            pltpu.VMEM((count, groups * room), bf16),
            pltpu.VMEM((count, groups * room), bf16),
        ]
    args += list(source) + list(after)
    specs += [VM] * len(source) + [ANY] * len(after)
    got = pl.pallas_call(
        functools.partial(forward_kernel, (depth, groups, capacity, room, norm_eps, len(after))),
        out_shape=outs,
        in_specs=specs,
        out_specs=[VM] * len(outs),
        scratch_shapes=scratch,
        compiler_params=pltpu.CompilerParams(**PARAMS),
        cost_estimate=pl.CostEstimate(
            flops=6 * 10**9, bytes_accessed=20 * 10**6, transcendentals=4 * 10**6
        ),
        name="layer_forward",
    )(*args)
    return list(got)


def expert_kernel(static, *refs):
    sizes, pairs, room, back, n_after = static
    refs = list(refs)
    take = lambda n: [refs.pop(0) for _ in range(n)]
    n = len(sizes)
    parts = take(n)
    row_blocks = take(pairs + 1)
    if back:
        grad_blocks = take(pairs + 1)
    take(n_after)
    near, crossed = take(2)
    if back:
        grad_parts = take(n)
    w, sems, row_sems, rows = take(4)
    if back:
        (grads,) = take(1)
    (acc,) = take(1)

    def bring(source, to, sem):
        out = [
            pltpu.make_async_copy(source[i].at[0:room], to.at[i * room : (i + 1) * room], sem.at[i])
            for i in range(pairs)
        ]
        rest = pl.ds(pairs * room, pairs * room)
        return out + [pltpu.make_async_copy(source[pairs], to.at[rest], sem.at[pairs])]

    first = bring(row_blocks, rows, row_sems.at[0])
    if back:
        first += bring(grad_blocks, grads, row_sems.at[1])
    starts = [sum(sizes[:i]) for i in range(n)]
    loads = [
        pltpu.make_async_copy(parts[i], w.at[:, pl.ds(starts[i], sizes[i]), :], sems.at[i])
        for i in range(n)
    ]
    for c in first + loads:
        c.start()
    for c in first:
        c.wait()
    turns = []
    for i in range(n):
        if not turns or sum(sizes[j] for j in turns[-1]) >= 256:
            turns.append([])
        turns[-1].append(i)
    for turn, members in enumerate(turns):
        for i in members:
            loads[i].wait()
        here = pl.ds(starts[members[0]], sum(sizes[i] for i in members))
        gate = dot_nt(rows[...], w[0, here, :])
        up = dot_nt(rows[...], w[1, here, :])
        sigmoid = 1.0 / (1.0 + jnp.exp(-gate))
        act = gate * sigmoid
        hidden = (act * up).astype(bf16)
        if back:
            grad_hidden = dot_nt(grads[...], w[2, here, :])
            grad_up = (grad_hidden * act).astype(bf16)
            grad_gate = (
                grad_hidden * up * (sigmoid * (1.0 + gate * (1.0 - sigmoid)))
            ).astype(bf16)
            y = dot(grad_gate, w[0, here, :]) + dot(grad_up, w[1, here, :])
            kinds = (
                dot_tn(grad_gate, rows[...]).astype(bf16),
                dot_tn(grad_up, rows[...]).astype(bf16),
                dot_tn(hidden, grads[...]).astype(bf16),
            )
            for kind in range(3):
                for i in members:
                    begin = starts[i] - starts[members[0]]
                    grad_parts[i][kind] = kinds[kind][begin : begin + sizes[i], :]
        else:
            y = dot(hidden, w[2, here, :])
        if turn > 0:
            y = acc[...] + y
        if turn < len(turns) - 1:
            acc[...] = y
        else:
            near[...] = y[: pairs * room].astype(bf16)
            crossed[...] = y[pairs * room :].astype(bf16)


def run_expert(parts, row_blocks, grad_blocks, room, after=()):
    width = row_blocks[0].shape[1]
    sizes = tuple(p.shape[1] for p in parts)
    n, pairs = len(parts), len(row_blocks) - 1
    count = 2 * pairs * room
    sds = jax.ShapeDtypeStruct
    back = grad_blocks is not None
    args = [*parts, *row_blocks, *(grad_blocks or []), *after]
    outs = [sds((pairs * room, width), bf16)] * 2
    outs += [sds(p.shape, bf16) for p in parts] if back else []
    low = pltpu.VMEM((count, width), bf16)
    scratch = [
        pltpu.VMEM((3, sum(sizes), width), bf16),
        pltpu.SemaphoreType.DMA((n,)),
        pltpu.SemaphoreType.DMA((2, pairs + 1)),
    ]
    scratch += [low] * (1 + int(back)) + [pltpu.VMEM((count, width), f32)]
    work = 6 * count * sum(sizes) * width * (3 if back else 1)
    got = pl.pallas_call(
        functools.partial(expert_kernel, (sizes, pairs, room, back, len(after))),
        out_shape=outs,
        in_specs=[ANY] * len(args),
        out_specs=[VM] * len(outs),
        scratch_shapes=scratch,
        compiler_params=pltpu.CompilerParams(**PARAMS),
        cost_estimate=pl.CostEstimate(
            flops=work, bytes_accessed=12 * 10**6, transcendentals=count * sum(sizes)
        ),
        name="expert",
    )(*args)
    return got[0], got[1], list(got[2:])


def fold_matrix(routed, width):
    a = lax.broadcasted_iota(jnp.int32, (LANES, LANES), 0)
    b = lax.broadcasted_iota(jnp.int32, (LANES, LANES), 1)
    return jnp.where((a % width) + routed == b, 1.0, 0.0).astype(bf16)


def row_picks(count, per):
    a = lax.broadcasted_iota(jnp.int32, (count, count // per), 0)
    b = lax.broadcasted_iota(jnp.int32, (count, count // per), 1)
    return jnp.where(a // per == b, 1.0, 0.0).astype(bf16)


def own_lanes(count, width):
    a = lax.broadcasted_iota(jnp.int32, (count, LANES), 0)
    b = lax.broadcasted_iota(jnp.int32, (count, LANES), 1)
    return (a % (LANES // width)) == (b // width)


def unpack_kernel(static, *refs):
    depth, routed, width, tiles, plan, n_after = static
    refs = list(refs)
    take = lambda n: [refs.pop(0) for _ in range(n)]
    (ints,) = take(1)
    parts = take(2 * len(plan))
    if depth > 0:
        (head_in,) = take(1)
    take(n_after)
    w_out, small_out, vecs_out, wg_out = take(4)
    if depth == 0:
        (head_out,) = take(1)
    flat, wide, deep, sems = take(4)
    me = ints[2]
    skip = 4 if depth > 0 else 0
    copies = []
    if depth > 0:
        copies.append(pltpu.make_async_copy(head_in, flat.at[0:4], sems.at[len(plan), 0]))
    for t, (axes, start, size) in enumerate(plan):
        for c in range(2):
            for j in range(8):
                away = c + sum(
                    AXIS_VALUE[axis] * ((j >> bit) & 1)
                    for bit, axis in enumerate(axes)
                )
                to = (me ^ away) * tiles + start + skip
                copies.append(
                    pltpu.make_async_copy(
                        parts[2 * t + c].at[j], flat.at[pl.ds(to, size)], sems.at[t, 8 * c + j]
                    )
                )
    for c in copies:
        c.start()
    for c in copies:
        c.wait()
    per = width // LANES
    size = width * per
    base = 4 * size // 8
    for i in range(4):

        def lift(r):
            s = pl.ds(i * size // 8 + r // 8, 12)
            wide[pl.ds(r, 96), :] = flat[s].astype(f32).reshape(96, LANES)

        blocks(size, 96, lift)
        for c in range(per):
            w_out[i, :, c * LANES : (c + 1) * LANES] = wide[
                pl.ds(c, width, stride=per), :
            ].astype(bf16)
    deep[...] = flat[pl.ds(base, deep.shape[0] // 8)].astype(f32).reshape(deep.shape)
    if depth == 0:
        head_out[...] = flat[pl.ds(base + 12, 4)]
    small = jnp.zeros((width, LANES), f32)
    at = 0
    for kinds, first in ((routed, 0), (4, MIX)):
        lines = width * kinds // LANES
        spread = dot(row_picks(width, LANES // kinds), deep[at : at + lines, :].astype(bf16))
        spread = jnp.where(own_lanes(width, kinds), spread, 0.0).astype(bf16)
        small = small + dot(spread, fold_matrix(first, kinds))
        at += lines
    small_out[...] = small.astype(bf16)
    vecs_out[...] = jnp.zeros(vecs_out.shape, f32)
    for r in range(4):
        for c in range(per):
            vecs_out[r : r + 1, c * LANES : (c + 1) * LANES] = deep[at : at + 1, :]
            at += 1
    a = lax.broadcasted_iota(jnp.int32, (LANES, LANES), 0)
    b = lax.broadcasted_iota(jnp.int32, (LANES, LANES), 1)
    if depth > 0:
        line = jnp.broadcast_to(deep[at : at + 1, :], (LANES, LANES))
        line = jnp.where((a == b // routed) & (a < routed), line, 0.0).astype(bf16)
        wg_out[...] = dot(line, fold_matrix(0, routed)).astype(bf16)
    else:
        wg_out[...] = jnp.zeros((LANES, LANES), bf16)


def unpack_layer(ints, parts, plan, head, depth, routed, width, tiles, after=()):
    sds = jax.ShapeDtypeStruct
    per = width // LANES
    outs = [
        sds((4, width, width), bf16),
        sds((width, LANES), bf16),
        sds((8, width), f32),
        sds((LANES, LANES), bf16),
    ]
    args = [ints, *parts]
    if depth > 0:
        args.append(head)
    args += list(after)
    if depth == 0:
        outs.append(sds((4, 8, LANES), bf16))
    got = pl.pallas_call(
        functools.partial(unpack_kernel, (depth, routed, width, tiles, plan, len(after))),
        out_shape=outs,
        in_specs=[SM] + [ANY] * (len(args) - 1),
        out_specs=[VM] * len(outs),
        scratch_shapes=[
            pltpu.VMEM((16 * tiles + 4, 8, LANES), bf16),
            pltpu.VMEM((width * per, LANES), f32),
            pltpu.VMEM((128 if depth == 0 else 104, LANES), f32),
            pltpu.SemaphoreType.DMA((len(plan) + 1, 16)),
        ],
        compiler_params=pltpu.CompilerParams(**PARAMS),
        cost_estimate=pl.CostEstimate(flops=10**9, bytes_accessed=10**7, transcendentals=0),
        name="unpack",
    )(*args)
    return dict(zip(("w", "small", "vecs", "wg"), got[:4])), list(got[4:])


def backward_kernel(static, *refs):
    depth, last, groups, room, packs, tiles, plan, n_after = static
    refs = list(refs)
    take = lambda n: [refs.pop(0) for _ in range(n)]
    (ints, grad_in, w_hbm, small, vecs, wg, cos, sin, side, routes, stream, n1, q_in, k_in, v_in) = take(15)
    mixed, lse, middle = take(3)
    back = take(groups)
    back_g = take(groups)
    if not last:
        (grad_side,) = take(1)
    if depth > 0:
        side_low, routes_low = take(2)
    elif packs:
        (head,) = take(1)
    take(n_after)
    if packs:
        flat_outs = take(2 * len(plan))
    else:
        (flat,) = take(1)
    grad_out, gains = take(2)
    if last:
        (output,) = take(1)
    if depth > 0:
        (grad_carry,) = take(1)
        send = take(groups // 2)
        if packs:
            (head_out,) = take(1)
    if not packs:
        small_out, wg_out = take(2)
    (w, bias, n2h, n2l, table, table_g, hot0, hot1, dn2, gm, gb, dmix, dq, dk, dv, acc, wide, acc_k, acc_v, sems) = take(20)
    if packs:
        flat, flat_sems = take(2)
    count, width = n1.shape
    routed = groups + 4
    per = width // LANES
    size = width * per
    rows = groups * room
    order = (3, 0, 1, 2)
    loads = [pltpu.make_async_copy(w_hbm.at[i], w.at[i], sems.at[i]) for i in range(4)]
    for i in order:
        loads[i].start()
    visible_bias(bias, ints[0], True)
    cols = Columns(side[...], routes[...], groups)
    lane = cols.lane
    g = cols.gates

    add_tables(back, table, room)
    add_tables(back_g, table_g, room)
    at = lax.broadcasted_iota(jnp.int32, (count, rows), 1).astype(f32)
    hot0[...] = jnp.where(at == cols.slots[0], 1.0, 0.0).astype(bf16)
    hot1[...] = jnp.where(at == cols.slots[1], 1.0, 0.0).astype(bf16)
    acc[...] = jnp.zeros(acc.shape, f32)

    def gather(c):
        s = pl.ds(c, LANES)
        grad = grad_in[:, s]
        m = middle[:, s]
        normed = m * cols.inverse_two * vecs[3:4, s]
        high, rest = split(normed)
        n2h[:, s] = high
        n2l[:, s] = rest
        p0 = dot(hot0[...], table[:, s])
        p1 = dot(hot1[...], table[:, s])
        if last:
            y = m + g[0] * p0 + g[1] * p1 + cols.normed_part * normed
            y = y + cols.constant_part[0] * vecs[0:1, s] + cols.constant_part[1] * vecs[1:2, s]
            output[:, s] = y.astype(bf16)
        acc[0] += grad * p0
        acc[1] += grad * p1
        acc[2] += grad * normed
        acc[3] += grad * vecs[0:1, s]
        acc[4] += grad * vecs[1:2, s]
        dn2[:, s] = dot(hot0[...] + hot1[...], table_g[:, s])

    blocks(width, LANES, gather)
    sums = [jnp.sum(acc[i], axis=1, keepdims=True) for i in range(5)]
    on_normed, on_first, on_second = sums[2:]
    by_special = [
        None,
        on_normed,
        cols.first[0] * on_normed + cols.first[1] * on_first,
        cols.second[0] * on_normed + cols.second[1] * on_second,
    ]
    grad_gates = []
    for k in range(2):
        total = sums[k]
        for j in range(1, 4):
            total = total + jnp.where(cols.routes[k] == groups + j, by_special[j], 0.0)
        grad_gates.append(total)
    inner = g[0] * grad_gates[0] + g[1] * grad_gates[1]
    lanes_grad = jnp.zeros((count, LANES), f32)
    for k in range(2):
        lanes_grad = lanes_grad + jnp.where(cols.hot[k], g[k] * (grad_gates[k] - inner), 0.0)
    if not last:
        lanes_grad = lanes_grad + grad_side[...]
    logit_grad = lanes_grad
    for pair, special, constant, first in (
        (cols.first, cols.special[2], on_first, MIX),
        (cols.second, cols.special[3], on_second, MIX + 2),
    ):
        left, right = special * on_normed, special * constant
        middle_sum = pair[0] * left + pair[1] * right
        lanes_grad = lanes_grad + jnp.where(lane == first, pair[0] * (left - middle_sum), 0.0)
        lanes_grad = lanes_grad + jnp.where(lane == first + 1, pair[1] * (right - middle_sum), 0.0)
    high, rest = split(lanes_grad)
    mix_high = jnp.where(lane >= MIX, lanes_grad, 0.0).astype(bf16)
    grad_small = dot_tn(n2h[...], high) + dot_tn(n2h[...], rest) + dot_tn(n2l[...], mix_high)
    if depth > 0:
        lh, lr = split(jnp.where(lane < routed, logit_grad, 0.0))
        grad_carry[...] = jnp.where(lane < routed, dot_nt(lh, wg[...]) + dot_nt(lr, wg[...]), 0.0)
        held = jnp.where(lane < routed, side_low[...], 0.0)
        hh, hr = split(held)
        grad_wg = dot_tn(hh, lh) + dot_tn(hh, lr) + dot_tn(hr, lh)

    def to_middle(c):
        s = pl.ds(c, LANES)
        y = dn2[:, s] + dot_nt(high, small[s, :]) + dot_nt(rest, small[s, :])
        dn2[:, s] = y + grad_in[:, s] * cols.normed_part

    blocks(width, LANES, to_middle)
    acc[0] = jnp.where(lane == 0, cols.constant_part[0], 0.0) + jnp.where(
        lane == 1, cols.constant_part[1], 0.0
    )
    zero = jnp.zeros((8, width), f32)

    def fold(v):
        return jnp.sum(v.reshape(v.shape[0] // 8, 8, width), axis=0)

    def back_norm(i, carry):
        d_gain, d_first, d_second = carry
        s = pl.ds(pl.multiple_of(i * 32, 32), 32)
        ln = lane_of(32)
        inverse = take_lane(side[s, :], ln, INV + 1)
        c0 = take_lane(acc[0, s, :], ln, 0)
        c1 = take_lane(acc[0, s, :], ln, 1)
        x = middle[s, :]
        d = dn2[s, :]
        grad = grad_in[s, :]
        d_gain = d_gain + fold(d * x * inverse)
        d_first = d_first + fold(grad * c0)
        d_second = d_second + fold(grad * c1)
        scaled = d * vecs[3:4, :]
        mean = jnp.mean(x * scaled, axis=1, keepdims=True)
        total = grad + inverse * scaled - x * (inverse * inverse * inverse * mean)
        gm[s, :] = total
        gb[s, :] = total.astype(bf16)
        return d_gain, d_first, d_second

    d_gain, d_first, d_second = lax.fori_loop(0, count // 32, back_norm, (zero, zero, zero))
    line = lambda v: jnp.sum(v, axis=0, keepdims=True)
    gain_two = line(d_gain)
    first_line, second_line = line(d_first), line(d_second)
    loads[3].wait()

    pending = []
    ready = []
    skip = 4 if depth > 0 else 0

    def send_flat(begin, end):
        ready.append((begin, end))
        for shard in range(16):
            low, high = shard * tiles + skip, (shard + 1) * tiles + skip
            covered = sum(max(0, min(high, e) - max(low, b)) for b, e in ready)
            if covered < tiles or shard in pending:
                continue
            pending.append(shard)
            for t in range(len(plan)):
                away_core = (ints[2] ^ shard) & 1
                for c in range(2):

                    @pl.when(away_core == c)
                    def _():
                        flat_copy(shard, t, c).start()

    def flat_copy(shard, t, c):
        away = ints[2] ^ shard
        axes, begin, size = plan[t]
        to = sum(((away // AXIS_VALUE[axis]) & 1) << bit for bit, axis in enumerate(axes))
        source = flat.at[pl.ds(shard * tiles + skip + begin, size)]
        return pltpu.make_async_copy(source, flat_outs[2 * t + c].at[to], flat_sems.at[t, shard])

    def write_flat(i):
        def lower(r):
            s = pl.ds(i * size // 8 + r // 8, 4)
            flat[s] = wide[pl.ds(r, 32), :].reshape(4, 8, LANES).astype(bf16)

        blocks(size, 32, lower)
        if packs:
            send_flat(i * size // 8, (i + 1) * size // 8)

    def weight_grad(i, left, right):
        def piece(c):
            y = dot_tn(left[...], right[:, pl.ds(c, LANES)])
            wide[pl.ds(c // LANES, width, stride=per), :] = y

        blocks(width, LANES, piece)
        write_flat(i)

    weight_grad(3, mixed, gb)

    def to_mixed(c):
        s = pl.ds(c, 256)
        dmix[:, s] = dot_nt(gb[...], w[3, s, :]).astype(bf16)

    blocks(width, 256, to_mixed)
    half_rows = count // 2

    def attend_pair(c):
        t = pl.ds(c, LANES)
        pair = c // LANES
        acc_k[...] = jnp.zeros(acc_k.shape, f32)
        acc_v[...] = jnp.zeros(acc_v.shape, f32)
        for qb in range(2):
            qs = pl.ds(qb * half_rows, half_rows)
            span = (qb + 1) * half_rows
            q2, do2 = q_in[qs, t], dmix[qs, t]
            k2, v2 = k_in[0:span, t], v_in[0:span, t]
            got = None
            for hd in range(2):
                mask = half_mask(hd)
                own = lambda v: v * mask

                km, qm, dom = own(k2), own(q2), own(do2)
                st = dot_nt(km, q2) + bias[0:span, qs]
                pt = jnp.exp(st - lse[pl.ds(2 * pair + hd, 1), qs])
                dpt = dot_nt(v2, dom)
                delta = jnp.sum(pt * dpt, axis=0, keepdims=True)
                dst = (pt * (dpt - delta)).astype(bf16)
                acc_v[0:span, :] += dot(pt.astype(bf16), dom)
                acc_k[0:span, :] += dot(dst, qm)
                y = dot_tn(dst, km)
                got = y if got is None else got + y
            ln = lane_of(half_rows)
            dq[qs, t] = rope_turn(got * 0.125, cos[qs, :], -sin[qs, :], ln).astype(bf16)
        dk[:, t] = rope_turn(acc_k[...], cos[...], -sin[...], lane).astype(bf16)
        dv[:, t] = acc_v[...].astype(bf16)

    blocks(width, LANES, attend_pair)
    for i, right in ((0, dq), (1, dk), (2, dv)):
        loads[i].wait()
    def to_normed(c):
        s = pl.ds(c, 256)
        y = dot_nt(dq[...], w[0, s, :]) + dot_nt(dk[...], w[1, s, :])
        dn2[:, s] = y + dot_nt(dv[...], w[2, s, :])

    blocks(width, 256, to_normed)

    def back_first(i, d_gain):
        s = pl.ds(pl.multiple_of(i * 32, 32), 32)
        inverse = take_lane(side[s, :], lane_of(32), INV)
        x = stream[s, :].astype(f32)
        d = dn2[s, :]
        d_gain = d_gain + fold(d * x * inverse)
        scaled = d * vecs[2:3, :]
        mean = jnp.mean(x * scaled, axis=1, keepdims=True)
        grad_out[s, :] = gm[s, :] + inverse * scaled - x * (inverse * inverse * inverse * mean)
        return d_gain

    gain_one = line(lax.fori_loop(0, count // 32, back_first, zero))
    gains[...] = jnp.zeros(gains.shape, f32)
    gains[0:1, :] = gain_one
    gains[1:2, :] = gain_two
    gains[2:3, :] = first_line
    gains[3:4, :] = second_line
    if depth > 0:
        low_cols = Columns(side_low[...], routes_low[...], groups)
        turned = jnp.transpose(side_low[...])
        at_t = lax.broadcasted_iota(jnp.int32, (rows, count), 0).astype(f32)
        is0 = at_t == turned[SLOT : SLOT + 1, :]
        is1 = at_t == turned[SLOT + 1 : SLOT + 2, :]
        put_grads(low_cols.gates, is0, is1, grad_out, send, room)
    for i, right in ((0, dq), (1, dk), (2, dv)):
        weight_grad(i, n1, right)
    if not packs:
        small_out[...] = grad_small.astype(bf16).astype(f32)
        low_wg = grad_wg.astype(bf16) if depth > 0 else jnp.zeros(wg_out.shape, bf16)
        wg_out[...] = low_wg.astype(f32)
        return
    tail = wide
    start = 0
    small_low = grad_small.astype(bf16)
    for kinds, first in ((routed, 0), (4, MIX)):
        lines = width * kinds // LANES
        spread = dot_nt(small_low, fold_matrix(first, kinds))
        spread = jnp.where(own_lanes(width, kinds), spread, 0.0).astype(bf16)
        tail[start : start + lines, :] = dot_tn(row_picks(width, LANES // kinds), spread)
        start += lines
    for row in (first_line, second_line, gain_one, gain_two):
        for c in range(per):
            tail[start : start + 1, :] = row[:, c * LANES : (c + 1) * LANES]
            start += 1
    used = 4 * size // 8 + start // 8
    flat[pl.ds(4 * size // 8, start // 8)] = (
        tail[0:start, :].reshape(start // 8, 8, LANES).astype(bf16)
    )
    a = lax.broadcasted_iota(jnp.int32, (8, LANES), 0)
    if depth > 0:
        ra = lax.broadcasted_iota(jnp.int32, (LANES, LANES), 0)
        rb = lax.broadcasted_iota(jnp.int32, (LANES, LANES), 1)
        spread = dot_nt(grad_wg.astype(bf16), fold_matrix(0, routed))
        spread = jnp.where((ra == rb // routed) & (ra < routed), spread, 0.0)
        one = jnp.sum(spread, axis=0, keepdims=True)
        flat[pl.ds(used, 1)] = jnp.where(a == 0, one, 0.0).reshape(1, 8, LANES).astype(bf16)
        left = flat.shape[0] - used - 1
        if left > 0:
            flat[pl.ds(used + 1, left)] = jnp.zeros((left, 8, LANES), bf16)
        head_out[...] = flat[0:4]
    else:
        flat[pl.ds(used, 4)] = head[...]
    send_flat(4 * size // 8, flat.shape[0])
    for t in range(len(plan)):
        for shard in range(16):
            flat_copy(shard, t, shard % 2).wait()


def layer_backward(
    depth, sizes, ints, grad_in, weights, tables, held, tabs, extra, packs, tiles, plan, after=()
):
    groups, room = sizes
    last = depth == LAYERS - 1
    count, width = held["n1"].shape
    rows = groups * room
    per = width // LANES
    sds = jax.ShapeDtypeStruct
    args = [
        ints, grad_in, weights["w"], weights["small"], weights["vecs"], weights["wg"], *tables,
        held["side"], held["routes"], held["stream"], held["n1"], held["q"], held["k"], held["v"],
        held["mixed"], held["lse"], held["middle"], *tabs, *extra,
    ]
    specs = [SM, VM, ANY] + [VM] * (len(args) - 3) + [ANY] * len(after)
    args += list(after)
    if packs:
        outs = [sds((8, size, 8, LANES), bf16) for _, _, size in plan for c in range(2)]
    else:
        outs = [sds((4 * width * per // 8, 8, LANES), bf16)]
    out_specs = [ANY if packs else VM] * len(outs)
    outs += [sds((count, width), f32), sds((8, width), f32)]
    if last:
        outs.append(sds((count, width), bf16))
    if depth > 0:
        outs += [sds((count, LANES), f32)] + [sds((2 * room, width), bf16)] * (groups // 2)
        if packs:
            outs.append(sds((4, 8, LANES), bf16))
    if not packs:
        outs += [sds((width, LANES), f32), sds((LANES, LANES), f32)]
    out_specs += [VM] * (len(outs) - len(out_specs))
    low = pltpu.VMEM((count, width), bf16)
    full = pltpu.VMEM((count, width), f32)
    side = pltpu.VMEM((count, LANES), f32)
    hot = pltpu.VMEM((count, rows), bf16)
    tab = pltpu.VMEM((rows, width), bf16)
    scratch = [
        pltpu.VMEM((4, width, width), bf16), pltpu.VMEM((count, count), f32), low, low, tab, tab, hot, hot,
        full, full, low, low, low, low, low, pltpu.VMEM((5, count, LANES), f32),
        pltpu.VMEM((width * per, LANES), f32), side, side, pltpu.SemaphoreType.DMA((4,)),
    ]
    if packs:
        scratch.append(pltpu.VMEM((16 * tiles + (4 if depth > 0 else 0), 8, LANES), bf16))
        scratch.append(pltpu.SemaphoreType.DMA((len(plan), 16)))
    got = pl.pallas_call(
        functools.partial(backward_kernel, (depth, last, groups, room, packs, tiles, plan, len(after))),
        out_shape=outs,
        in_specs=specs,
        out_specs=out_specs,
        scratch_shapes=scratch,
        compiler_params=pltpu.CompilerParams(**PARAMS),
        cost_estimate=pl.CostEstimate(
            flops=14 * 10**9, bytes_accessed=30 * 10**6, transcendentals=4 * 10**6
        ),
        name="layer_backward",
    )(*args)
    return list(got)


def rope_tables(count):
    lane = np.arange(LANES)
    frequency = rope_base ** (-(lane % 32).astype(np.float32) / np.float32(32))
    angle = np.arange(count, dtype=np.float32)[:, None] * frequency[None, :].astype(np.float32)
    sign = np.where(lane % 64 < 32, -1.0, 1.0)
    cos, sin = np.cos(angle), np.sin(angle) * sign[None, :]
    return jnp.asarray(cos.astype(np.float32)), jnp.asarray(sin.astype(np.float32))


def unpack_plain(flat, routed, width):
    params = [dict() for depth in range(LAYERS)]
    params = unpack(flat, width, routed)
    out = []
    for p in params:
        small = jnp.zeros((width, LANES), bf16)
        small = small.at[:, :routed].set(p["router"]).at[:, MIX : MIX + 4].set(p["mixing"])
        vecs = jnp.zeros((8, width), f32)
        vecs = vecs.at[0:2].set(p["constant"].astype(f32))
        vecs = vecs.at[2].set(p["attn_gain"].astype(f32)).at[3].set(p["moe_gain"].astype(f32))
        wg = jnp.zeros((LANES, LANES), bf16)
        if "carry" in p:
            wg = wg.at[:routed, :routed].set(p["carry"])
        w = jnp.stack([p[n] for n in ("query", "key", "value", "output")])
        out.append(dict(w=w, small=small, vecs=vecs, wg=wg))
    return out


def on_device(
    tokens_in,
    cotangent,
    seq_lengths,
    drop_order,
    routes,
    dense_master,
    dense_moment,
    dense_second,
    expert_master,
    expert_moment,
    expert_second,
):
    count, width = tokens_in.shape
    wires = Wires()
    groups = wires.groups
    routed = groups + 4
    capacity = max(2, 45 * count // (32 * routed))
    room = -(-capacity // 16) * 16
    sizes = (groups, capacity, room)
    whole_size = dense_master.shape[0] * wires.dp * groups
    order = drop_order[0]
    place = (wires.me_dp % 4) * 4 + wires.me_group
    ints = jnp.stack([seq_lengths[0], wires.me_group.astype(jnp.int32), place.astype(jnp.int32)])
    tables = rope_tables(count)
    tiles = dense_master.shape[0] // (8 * LANES)
    packs = (
        LANES % routed == 0
        and (wires.tops, groups) == (2, 4)
        and dense_master.shape[0] == tiles * 8 * LANES
    )
    bsizes = (groups, room)
    half = groups // 2
    thirds, halves = plan_thirds(tiles), plan_halves(tiles)

    dense_low = dense_master.astype(bf16)
    expert_low = [expert_master[0, depth].astype(bf16) for depth in range(LAYERS)]
    far = range(1, wires.tops)
    if packs:
        shard = dense_low.reshape(tiles, 8, LANES)
        top = wires.me_dp >= 4
        other = wires.swap(shard, h=1)
        pieces = [jnp.where(top, other, shard), jnp.where(top, shard, other)]
        dense0 = [pieces[0][None, a : a + n] for _, a, n in thirds]
        for step in range(3):
            dense0 = grow(wires, dense0, thirds, step)
            if step == 0:
                whole = pin(pieces[1][None], dense0)
                dense1 = jnp.concatenate([whole, wires.swap(whole, l=1)], axis=0)
        go = tuple(dense0)
        cores = [wires.swap(v, g=1) for v in dense0]
        parts = [v for pair in zip(dense0, cores) for v in pair]
        dense1 = [pin(dense1, *go)[:, a : a + n] for _, a, n in halves]
        dense1 = grow(wires, dense1, halves, 1)
        first, (head,) = unpack_layer(ints, parts, thirds, None, 0, routed, width, tiles)
    else:
        full = lax.all_gather(dense_low, ALL, axis=0, tiled=True)
        first, second = unpack_plain(full, routed, width)
        go = (first["vecs"],)
    expert_low[0] = pin(expert_low[0], *go)
    got_far = [wires.swap(v, h=h) for h in far for v in cut_far(expert_low[0])]
    near = wires.swap(expert_low[0], x=1)

    names = ("n1", "q", "k", "v", "mixed", "lse", "middle", "side", "stream")
    got = layer_forward(0, sizes, ints, order, routes[0], first, [tokens_in], tables)
    held0 = dict(zip(names, got[half:]), stream=tokens_in, routes=routes[0])
    gone = held0["side"]
    cross_far = [wires.swap(pin(v, gone), x=1) for v in got_far[:-1]]
    if packs:
        dense1 = grow(wires, [pin(v, gone) for v in dense1], halves, 2)
    arrived0 = exchange_out(wires, got[:half])
    cross_far.append(wires.swap(pin(got_far[-1], arrived0[1]), x=1))
    expert0 = [expert_low[0], near]
    for pair in zip(got_far, cross_far):
        expert0 += list(pair)
    low1 = pin(cut_far(expert_low[1]), *arrived0)
    got_far1 = [wires.swap(low1[0], h=h) for h in far]
    near0, crossed0, _ = run_expert(expert0, arrived0, None, room)
    near1 = wires.swap(pin(expert_low[1], near0), x=1)
    ret0 = exchange_back(wires, near0, crossed0)
    if packs:
        dense1 = pin(dense1, near0)
        cores = [wires.swap(v, g=1) for v in dense1]
        parts = [v for pair in zip(dense1, cores) for v in pair]
        second, _ = unpack_layer(ints, parts, halves, head, 1, routed, width, tiles)
    weights = [first, second]
    low1 = pin(low1, *ret0)
    last_far1 = [wires.swap(low1[1], h=h) for h in far]
    cross_far1 = [wires.swap(pin(v, *ret0), x=1) for v in got_far1]

    source = [
        held0["side"], routes[0], held0["middle"], weights[0]["vecs"], weights[1]["wg"], cotangent, *ret0,
    ]
    got = layer_forward(1, sizes, ints, order, routes[1], second, source, tables)
    held1 = dict(zip(names, got[groups:]), routes=routes[1])
    arrived1 = exchange_out(wires, got[:half])
    last_cross1 = [wires.swap(pin(v, held1["side"]), x=1) for v in last_far1]
    expert1 = [expert_low[1], near1]
    for four in zip(got_far1, cross_far1, last_far1, last_cross1):
        expert1 += list(four)
    grads1 = exchange_out(wires, pin(got[half:groups], *arrived1))
    out1, crossed1, _ = run_expert(expert1, arrived1, None, room)
    ret1 = exchange_back(wires, out1, pin(crossed1, *grads1))
    out1, crossed1, parts1 = run_expert(expert1, arrived1, grads1, room)
    sum1 = ScatterExpert(wires, parts1)
    sum1.first()
    back1 = exchange_back(wires, out1, crossed1)
    sum1.second(*back1)

    got = layer_backward(
        1, bsizes, ints, cotangent, second, tables, held1, [*ret1, *back1],
        [held0["side"], routes[0]], packs, tiles, halves,
    )
    n_flat = 2 * len(halves) if packs else 1
    flat1, got = got[:n_flat], got[n_flat:]
    grad1, gains1, output, grad_side = got[:4]
    rest1 = got[4 + half :]
    if packs:
        dense1 = ScatterDense(wires, list(zip(flat1[0::2], flat1[1::2])), halves)
        dense1.send(0)
    grads0 = exchange_out(wires, pin(got[4 : 4 + half], *sum1.received()))
    if packs:
        dense1.add()
        dense1.send(1, *grads0)
    out0, crossed0, parts0 = run_expert(expert0, arrived0, grads0, room)
    sum0 = ScatterExpert(wires, parts0)
    sum0.first()
    back0 = exchange_back(wires, out0, crossed0)
    if packs:
        dense1.add()
        dense1.send(2, out0)
        dense1.add()
    sum0.second(*back0)
    extra = [grad_side]
    if packs:
        dense1.send(3, *back0)
        dense1.add()
        extra.append(rest1[0])

    got = layer_backward(
        0, bsizes, ints, grad1, first, tables, held0, [*ret0, *back0], extra,
        packs, tiles, thirds,
    )
    n_flat = 2 * len(thirds) if packs else 1
    flat0, got = got[:n_flat], got[n_flat:]
    grad_stream, gains0 = got[:2]
    flat0, *_ = pin(flat0, *sum0.received()), None
    shard1 = sum1.done()
    shard0 = sum0.done()
    if packs:
        dense0 = ScatterDense(wires, list(zip(flat0[0::2], flat0[1::2])), thirds)
        for step in range(4):
            dense0.send(step)
            dense0.add()
        both = [dense0.done(), dense1.done()]
        give = jnp.where(top, both[0], both[1])
        keep = jnp.where(top, both[1], both[0])
        dense_shard = keep.astype(f32) + wires.swap(give, h=1).astype(f32)
    else:
        pieces = []
        for flat, gains, (small, wg) in ((flat0[0], gains0, got[2:4]), (flat1[0], gains1, rest1)):
            pieces += [flat.reshape(-1), small[:, :routed].reshape(-1)]
            pieces += [small[:, MIX : MIX + 4].reshape(-1)]
            pieces += [gains[2:4].reshape(-1), gains[0:2].reshape(-1)]
        pieces.append(wg[:routed, :routed].reshape(-1))
        flat = jnp.concatenate([p.astype(bf16) for p in pieces])
        flat = jnp.concatenate([flat, jnp.zeros((whole_size - flat.shape[0],), bf16)])
        dense_shard = lax.psum_scatter(flat, ALL, scatter_dimension=0, tiled=True)
    dense_shard = dense_shard.astype(f32).reshape(-1)
    expert_shard = jnp.stack([shard0, shard1], axis=0)[None]
    gain_local = jnp.stack([gains0[0:2], gains1[0:2]], axis=0)
    local_square = jnp.sum(dense_shard * dense_shard) + jnp.sum(expert_shard * expert_shard)
    if packs:
        payload = jnp.concatenate([gain_local.reshape(4, width), jnp.zeros((4, width), f32)], axis=0)
        payload = payload.at[4].set(local_square)
        for step in (dict(g=1), dict(x=1), dict(g=2), dict(l=1), dict(h=1)):
            payload = payload + wires.swap(payload, **step)
        gain_total = payload[:4].reshape(2, 2, width)
        square_sum = payload[4, 0]
    else:
        square_sum, gain_total = lax.psum((local_square, gain_local), ALL)
    factor = jnp.minimum(1.0, clip_norm / (jnp.sqrt(square_sum) + 1e-06))
    dense_clip = dense_shard * factor
    expert_clip = expert_shard * factor
    dense_step = adam_delta(dense_master, dense_moment, dense_second, dense_clip)
    expert_step = adam_delta(expert_master, expert_moment, expert_second, expert_clip)
    return (
        output,
        grad_stream,
        dense_clip,
        expert_clip,
        gain_total * factor,
        dense_step,
        expert_step,
    )


def solution(mesh):
    return jax.shard_map(
        on_device,
        mesh=mesh,
        in_specs=(
            P(("dp", "group"), None),
            P(("dp", "group"), None),
            P(("dp", "group")),
            P(("dp", "group"), None),
            P(None, ("dp", "group"), None),
            P(("dp", "group")),
            P(("dp", "group")),
            P(("dp", "group")),
            P("group", None, None, "dp", None),
            P("group", None, None, "dp", None),
            P("group", None, None, "dp", None),
        ),
        out_specs=(
            P(("dp", "group"), None),
            P(("dp", "group"), None),
            P(("dp", "group")),
            P("group", None, None, "dp", None),
            P(),
            P(("dp", "group")),
            P("group", None, None, "dp", None),
        ),
        check_vma=False,
    )
```

time: 1730 us -> 681 us (0.39); the launches traced: 1700 us -> 677 us
  waiting for transfers between devices: 878 us -> 276 us
  local copies, waits for them, and re-layouts: 400 us -> 23.2 us
  Pallas kernels: 0 us -> 231 us
  matrix products: 179 us -> 0 us
  other arithmetic: 152 us -> 48.9 us
  starting transfers between devices: 30.9 us -> 92.9 us
  blocking collectives: 39.5 us -> 0 us
    reduce_scatter x2 -> x0, waiting for transfers between devices: 377 us -> none  [the longest x1 313 us: on_device(): lax.psum_scatter(jnp.concatenate(expert_grads, axis=1).astype(jnp.bfloat1...]
    all_gather x2 -> x0, waiting for transfers between devices: 330 us -> none  [the longest x1 265 us: on_device(): lax.all_gather(expert_master.astype(jnp.bfloat16), 'dp', axis=3, tiled=True)]
    ppermute x0 -> x98, waiting for transfers between devices: none -> 276 us  [swap(): return lax.ppermute(array, ALL, pairs)]
    pallas_call x0 -> x10, Pallas kernels: none -> 231 us  [the longest x2 106 us: layer_backward(): pl.pallas_call(functools.partial(backward_kernel, (depth, last, groups, r...]
    dot_general x71 -> x0, matrix products: 179 us -> none  [the longest x2 22.5 us: attend_back(): jnp.einsum('qhd,khd->hqk', grad_rows, values, preferred_element_type=jnp....]
    unnamed x6 -> x0, waiting for transfers between devices: 151 us -> none
    concatenate x5 -> x1, local copies, waits for them, and re-layouts: 149 us -> 0.61 us  [on_device(): jnp.concatenate([gain_local.reshape(4, width), jnp.zeros((4, width), f32)...]
    ppermute x0 -> x98, starting transfers between devices: none -> 92.9 us  [swap(): return lax.ppermute(array, ALL, pairs)]
  transfers between devices with their start and end apart: 13 -> 98, of which waited for: 8 -> 48; matrix products, arithmetic and copies ran while one was open for 13% -> 7% of each run, Pallas kernels for 0% -> 27%
where the time goes in v1:
time: 681 us; the launch traced here: 677 us
  waiting for transfers between devices  276 us (41%)
  Pallas kernels  231 us (34%)
  starting transfers between devices  92.9 us (14%)
  other arithmetic  48.9 us (7%)
  local copies, waits for them, and re-layouts  23.2 us (3%)
    ppermute x98, waiting for transfers between devices, swap(): return lax.ppermute(array, ALL, pairs)  276 us
    pallas_call x2, Pallas kernels, layer_backward(): pl.pallas_call(functools.partial(backward_kernel, (depth, last, groups, r...  106 us
    ppermute x98, starting transfers between devices, swap(): return lax.ppermute(array, ALL, pairs)  92.9 us
    pallas_call x2, Pallas kernels, layer_forward(): pl.pallas_call(functools.partial(forward_kernel, (depth, groups, capacity...  54.5 us
    pallas_call x4, Pallas kernels, run_expert(): pl.pallas_call(functools.partial(expert_kernel, (sizes, pairs, room, back...  51.5 us
    pallas_call x2, Pallas kernels, unpack_layer(): pl.pallas_call(functools.partial(unpack_kernel, (depth, routed, width, ti...  19.1 us
  transfers between devices with their start and end apart: 98, of which 48 were waited for; matrix products, arithmetic and copies ran while one was open for 7% of the time, Pallas kernels for 27%

profile of v1, /device:TPU:0, one launch (start us, length us, event | category | flops | bytes accessed | tf_op | source)
XLA Modules:
  0.0 677.0 jit_solution(17981612961262021572)
XLA Ops:
  1.8 4.1 collective-permute-start
  5.9 13.4 %collective-permute-done = bf16[145,8,128]{2,1,0:T(8,128)(2,1)S(1)} collective-permute-done((bf16[145,8,128]{2,1,0:T(8,128)(2,1)S(1)}, bf16[145,8,128]{2,1,0:T(8,128)(2,1)S(1)}, u32[]{:S(2)}, u32[]{:S(2)}) %collective-permute-start) | collective-permute-done | bytes 296992 | tf_op jit(solution)/shard_map/ppermute | solution.py:77
  31.1 2.5 collective-permute-done.9
  36.4 4.1 collective-permute-done.8
  47.3 2.6 convert.4
  54.6 3.1 collective-permute-start.21
  57.7 9.6 %unpack.2 = (bf16[4,768,768]{2,1,0:T(8,128)(2,1)}, bf16[768,128]{1,0:T(8,128)(2,1)}, f32[8,768]{1,0:T(8,128)}, bf16[128,128]{1,0:T(8,128)(2,1)}, bf16[4,8,128]{2,1,0:T(8,128)(2,1)}) custom-call(s32[3]{0:T(128)} %pad_add_fusion.refs_0_, bf16[8,49,8,128]{3,2,1,0:T(8,128)(2,1)} %pad_maximum_fusion.3.refs_1_, ...), custom_call_target="tpu_custom_call" | custom-call | flops 1000000000 | bytes 10000000 | tf_op jit(solution)/shard_map/unpack/pallas_call | solution.py:795
  67.3 23.0 %layer_forward.2 = (bf16[192,768]{1,0:T(8,128)(2,1)}, bf16[192,768]{1,0:T(8,128)(2,1)}, bf16[512,768]{1,0:T(8,128)(2,1)}, bf16[512,768]{1,0:T(8,128)(2,1)}, bf16...) custom-call(s32[3]{0:T(128)} %pad_add_fusion.refs_0_, ...), custom_call_target="tpu_custom_call" | custom-call | flops 6000000000 | bytes 20000000 | tf_op jit(solution)/shard_map/layer_forward/pallas_call | solution.py:559
  93.0 4.3 collective-permute-done.21.refs_4_
  98.0 11.2 %collective-permute-done.19.refs_2_ = bf16[3,128,768]{2,1,0:T(8,128)(2,1)} collective-permute-done((bf16[3,128,768]{2,1,0:T(8,128)(2,1)S(1)}, bf16[3,128,768]{2,1,0:T(8,128)(2,1)}, u32[]{:S(2)}, u32[]{:S(2)}) %collective-permute-start.19) | collective-permute-done | bytes 589856 | tf_op jit(solution)/shard_map/ppermute | solution.py:77
  112.2 3.9 collective-permute-done.25.refs_9_
  116.1 5.6 collective-permute-done.24.refs_8_
  124.6 19.7 %collective-permute-done.11 = bf16[2,73,8,128]{3,2,1,0:T(8,128)(2,1)S(1)} collective-permute-done((bf16[2,73,8,128]{3,2,1,0:T(8,128)(2,1)S(1)}, bf16[2,73,8,128]{3,2,1,0:T(8,128)(2,1)S(1)}, u32[]{:S(2)}, u32[]{:S(2)}) %collective-permute-start.11) | collective-permute-done | bytes 299040 | tf_op jit(solution)/shard_map/ppermute | solution.py:77
  148.9 8.7 %expert.4 = (bf16[384,768]{1,0:T(8,128)(2,1)}, bf16[384,768]{1,0:T(8,128)(2,1)}) custom-call(bf16[3,256,768]{2,1,0:T(8,128)(2,1)} %get-tuple-element.136.refs_0_, bf16[3,256,768]{2,1,0:T(8,128)(2,1)} %collective-permute-done.18.refs_1_, bf16[3,128,768]{2,1,0:T(8,128)(2,1)} %collective-permute-done.19.refs_2_, bf16[3,128,768]{2,1,0:T(8,128)(2,1)} %copy-done.43, ...), custom_call_target="tpu_custom_call" | custom-call | flops 3623878656 | bytes 12000000 | tf_op jit(solution)/shard_map/expert/pallas_call | solution.py:671
  170.7 9.5 %unpack.3 = (bf16[4,768,768]{2,1,0:T(8,128)(2,1)}, bf16[768,128]{1,0:T(8,128)(2,1)}, f32[8,768]{1,0:T(8,128)}, bf16[128,128]{1,0:T(8,128)(2,1)}) custom-call(s32[3]{0:T(128)} %pad_add_fusion.refs_0_, bf16[8,73,8,128]{3,2,1,0:T(8,128)(2,1)} %copy-done.2, bf16[8,73,8,128]{3,2,1,0:T(8,128)(2,1)} %copy-done.4, ...), custom_call_target="tpu_custom_call" | custom-call | flops 1000000000 | bytes 10000000 | tf_op jit(solution)/shard_map/unpack/pallas_call | solution.py:795
  180.2 31.6 %layer_forward.3 = (bf16[192,768]{1,0:T(8,128)(2,1)}, bf16[192,768]{1,0:T(8,128)(2,1)}, bf16[192,768]{1,0:T(8,128)(2,1)}, bf16[192,768]{1,0:T(8,128)(2,1)}, bf16...) custom-call(s32[3]{0:T(128)} %pad_add_fusion.refs_0_, ...), custom_call_target="tpu_custom_call" | custom-call | flops 6000000000 | bytes 20000000 | tf_op jit(solution)/shard_map/layer_forward/pallas_call | solution.py:559
  216.3 6.6 collective-permute-done.40.refs_9_
  222.9 3.7 collective-permute-done.38.refs_7_
  234.0 35.1 %collective-permute-done.34.refs_2_ = bf16[3,128,768]{2,1,0:T(8,128)(2,1)S(1)} collective-permute-done((bf16[3,128,768]{2,1,0:T(8,128)(2,1)S(1)}, bf16[3,128,768]{2,1,0:T(8,128)(2,1)S(1)}, u32[]{:S(2)}, u32[]{:S(2)}) %collective-permute-start.34) | collective-permute-done | bytes 589856 | tf_op jit(solution)/shard_map/ppermute | solution.py:77
  269.1 12.6 %collective-permute-done.36.refs_4_ = bf16[3,128,768]{2,1,0:T(8,128)(2,1)S(1)} collective-permute-done((bf16[3,128,768]{2,1,0:T(8,128)(2,1)S(1)}, bf16[3,128,768]{2,1,0:T(8,128)(2,1)S(1)}, u32[]{:S(2)}, u32[]{:S(2)}) %collective-permute-start.36) | collective-permute-done | bytes 589856 | tf_op jit(solution)/shard_map/ppermute | solution.py:77
  283.9 4.0 collective-permute-done.43.refs_13_
  288.1 9.8 %collective-permute-done.35.refs_3_ = bf16[3,128,768]{2,1,0:T(8,128)(2,1)S(1)} collective-permute-done((bf16[3,128,768]{2,1,0:T(8,128)(2,1)S(1)}, bf16[3,128,768]{2,1,0:T(8,128)(2,1)S(1)}, u32[]{:S(2)}, u32[]{:S(2)}) %collective-permute-start.35) | collective-permute-done | bytes 589856 | tf_op jit(solution)/shard_map/ppermute | solution.py:77
  297.9 11.6 %collective-permute-done.37.refs_5_ = bf16[3,128,768]{2,1,0:T(8,128)(2,1)S(1)} collective-permute-done((bf16[3,128,768]{2,1,0:T(8,128)(2,1)S(1)}, bf16[3,128,768]{2,1,0:T(8,128)(2,1)S(1)}, u32[]{:S(2)}, u32[]{:S(2)}) %collective-permute-start.37) | collective-permute-done | bytes 589856 | tf_op jit(solution)/shard_map/ppermute | solution.py:77
  310.3 16.9 %expert.6 = (bf16[384,768]{1,0:T(8,128)(2,1)}, bf16[384,768]{1,0:T(8,128)(2,1)}, bf16[3,256,768]{2,1,0:T(8,128)(2,1)}, bf16[3,256,768]{2,1,0:T(8,128)(2,1)}, bf1...) custom-call(bf16[3,256,768]{2,1,0:T(8,128)(2,1)} %get-tuple-element., ...), custom_call_target="tpu_custom_call" | custom-call | flops 10871635968 | bytes 12000000 | tf_op jit(solution)/shard_map/expert/pallas_call | solution.py:671
  327.4 9.0 %expert.5 = (bf16[384,768]{1,0:T(8,128)(2,1)}, bf16[384,768]{1,0:T(8,128)(2,1)}) custom-call(bf16[3,256,768]{2,1,0:T(8,128)(2,1)} %get-tuple-element.160.refs_0_, bf16[3,256,768]{2,1,0:T(8,128)(2,1)} %copy-done.42, bf16[3,128,768]{2,1,0:T(8,128)(2,1)} %copy-done.50, bf16[3,128,768]{2,1,0:T(8,128)(2,1)} %copy-done.52, bf16[3,128,768]{2,1,0:T(8,128)(2,1)} %copy-done.51, ...), custom_call_target="tpu_custom_call" | custom-call | flops 3623878656 | bytes 12000000 | tf_op jit(solution)/shard_map/expert/pallas_call | solution.py:671
  341.3 2.7 collective-permute-start.53
  345.1 4.3 collective-permute-done.51.refs_23_
  351.2 7.0 %collective-permute-done.53.refs_25_ = bf16[192,768]{1,0:T(8,128)(2,1)S(1)} collective-permute-done((bf16[192,768]{1,0:T(8,128)(2,1)S(1)}, bf16[192,768]{1,0:T(8,128)(2,1)S(1)}, u32[]{:S(2)}, u32[]{:S(2)}) %collective-permute-start.53) | collective-permute-done | bytes 294944 | tf_op jit(solution)/shard_map/ppermute | solution.py:77
  358.6 3.4 collective-permute-start.55
  362.1 4.0 collective-permute-done.56
  368.7 5.3 collective-permute-done.48.refs_20_
  374.1 4.9 collective-permute-done.49.refs_21_
  379.8 55.0 %layer_backward.2 = (bf16[8,73,8,128]{3,2,1,0:T(8,128)(2,1)}, bf16[8,73,8,128]{3,2,1,0:T(8,128)(2,1)}, bf16[8,72,8,128]{3,2,1,0:T(8,128)(2,1)}, bf16[8,72,8,128]...) custom-call(s32[3]{0:T(128)} %pad_add_fusion.refs_0_, ...), custom_call_target="tpu_custom_call" | custom-call | flops 14000000000 | bytes 30000000 | tf_op jit(solution)/shard_map/layer_backward/pallas_call | solution.py:1172
  439.3 6.6 collective-permute-done.61.refs_14_
  453.9 16.8 %expert.7 = (bf16[384,768]{1,0:T(8,128)(2,1)}, bf16[384,768]{1,0:T(8,128)(2,1)}, bf16[3,256,768]{2,1,0:T(8,128)(2,1)}, bf16[3,256,768]{2,1,0:T(8,128)(2,1)}, bf1...) custom-call(bf16[3,256,768]{2,1,0:T(8,128)(2,1)} %get-tuple-element., ...), custom_call_target="tpu_custom_call" | custom-call | flops 10871635968 | bytes 12000000 | tf_op jit(solution)/shard_map/expert/pallas_call | solution.py:671
  480.3 35.6 %collective-permute-done.72 = bf16[4,72,8,128]{3,2,1,0:T(8,128)(2,1)S(1)} collective-permute-done((bf16[4,72,8,128]{3,2,1,0:T(8,128)(2,1)S(1)}, bf16[4,72,8,128]{3,2,1,0:T(8,128)(2,1)S(1)}, u32[]{:S(2)}, u32[]{:S(2)}) %collective-permute-start.72) | collective-permute-done | bytes 589856 | tf_op jit(solution)/shard_map/ppermute | solution.py:77
  521.2 4.6 collective-permute-done.65.refs_24_
  526.5 4.3 collective-permute-done.66.refs_25_
  533.2 2.5 collective-permute-start.78
  536.9 50.8 %layer_backward.3 = (bf16[8,49,8,128]{3,2,1,0:T(8,128)(2,1)}, bf16[8,49,8,128]{3,2,1,0:T(8,128)(2,1)}, bf16[8,48,8,128]{3,2,1,0:T(8,128)(2,1)}, bf16[8,48,8,128]...) custom-call(s32[3]{0:T(128)} %pad_add_fusion.refs_0_, ...), custom_call_target="tpu_custom_call" | custom-call | flops 14000000000 | bytes 30000000 | tf_op jit(solution)/shard_map/layer_backward/pallas_call | solution.py:1172
  594.2 3.0 collective-permute-done.74
  605.3 7.9 %collective-permute-done.85 = bf16[4,48,8,128]{3,2,1,0:T(8,128)(2,1)S(1)} collective-permute-done((bf16[4,48,8,128]{3,2,1,0:T(8,128)(2,1)S(1)}, bf16[4,48,8,128]{3,2,1,0:T(8,128)(2,1)S(1)}, u32[]{:S(2)}, u32[]{:S(2)}) %collective-permute-start.85) | collective-permute-done | bytes 393248 | tf_op jit(solution)/shard_map/ppermute | solution.py:77
  616.5 2.6 collective-permute-done.86
  624.8 3.8 collective-permute-done.83
  634.6 5.0 collective-permute-done.92
  653.6 3.8 collective-permute-done.96
  657.8 4.4 collective-permute-done.97
  665.3 9.9 %fusion.6 = (f32[1,2,3,256,768]{4,3,2,1,0:T(8,128)}, f32[1,2,3,256,768]{4,3,2,1,0:T(8,128)}) fusion(f32[1,2,3,256,768]{4,3,2,1,0:T(8,128)} %param.23, f32[1,2,3,256,768]{4,3,2,1,0:T(8,128)} %param.25, f32[1,2,3,256,768]{4,3,2,1,0:T(8,128)} %param.24, f32[]{:T(128)} %bitcast.21, f32[1,1,3,256,768]{4,3,2,1,0:T(8,128)S(1)} %add_bitcast_fusion, ...), kind=kLoop, calls=%fused_computation.9 | loop fusion | flops 18874368 | bytes 28311556 | tf_op jit(solution)/shard_map/mul | solution.py:204
  (404 shorter events, 157.8 us)
Async XLA Ops:
  1.8 17.5 %collective-permute-start = (bf16[145,8,128]{2,1,0:T(8,128)(2,1)S(1)}, bf16[145,8,128]{2,1,0:T(8,128)(2,1)S(1)}, u32[]{:S(2)}, u32[]{:S(2)}) collective-permute-start(bf16[145,8,128]{2,1,0:T(8,128)(2,1)S(1)} %convert_bitcast_fusion), channel_id=1, source_target_pairs={{0,16},{1,17},{2,18},{3,19},{4,20},{5,21},{6,22},{7,23},{8,24},{9,... | collective-permute-start | bytes 890888 | tf_op jit(solution)/shard_map/ppermute | solution.py:77
  52.0 39.5 %collective-permute-start.4 = (bf16[1,145,8,128]{3,2,1,0:T(8,128)(2,1)S(1)}, bf16[1,145,8,128]{3,2,1,0:T(8,128)(2,1)S(1)}, u32[]{:S(2)}, u32[]{:S(2)}) collective-permute-start(bf16[1,145,8,128]{3,2,1,0:T(8,128)(2,1)S(1)} %get-tuple-element.128), channel_id=1, source_target_pairs={{0,8},{1,9},{2,10},{3,11},{4,12},{5,13},{6,14},{7,15},{8,0},{9,1},... | collective-permute-start | bytes 890888 | tf_op jit(solution)/shard_map/ppermute | solution.py:77
  52.3 93.1 %collective-permute-start.18 = (bf16[3,256,768]{2,1,0:T(8,128)(2,1)}, bf16[3,256,768]{2,1,0:T(8,128)(2,1)}, u32[]{:S(2)}, u32[]{:S(2)}) collective-permute-start(bf16[3,256,768]{2,1,0:T(8,128)(2,1)} %get-tuple-element.136.refs_0_), channel_id=1, source_target_pairs={{0,4},{1,5},{2,6},{3,7},{4,0},{5,1},{6,2},{7,3},{8,12},{9,13},{10,... | collective-permute-start | bytes 3538952 | tf_op jit(solution)/shard_map/ppermute | solution.py:77
  54.6 42.7 %collective-permute-start.21 = (bf16[3,128,768]{2,1,0:T(8,128)(2,1)S(1)}, bf16[3,128,768]{2,1,0:T(8,128)(2,1)}, u32[]{:S(2)}, u32[]{:S(2)}) collective-permute-start(bf16[3,128,768]{2,1,0:T(8,128)(2,1)S(1)} %get-tuple-element.259), channel_id=1, source_target_pairs={{0,16},{1,17},{2,18},{3,19},{4,20},{5,21},{6,22},{7,23},{8,24},{9,... | collective-permute-start | bytes 1769480 | tf_op jit(solution)/shard_map/ppermute | solution.py:77
  57.6 51.6 %collective-permute-start.19 = (bf16[3,128,768]{2,1,0:T(8,128)(2,1)S(1)}, bf16[3,128,768]{2,1,0:T(8,128)(2,1)}, u32[]{:S(2)}, u32[]{:S(2)}) collective-permute-start(bf16[3,128,768]{2,1,0:T(8,128)(2,1)S(1)} %get-tuple-element.260), channel_id=1, source_target_pairs={{0,16},{1,17},{2,18},{3,19},{4,20},{5,21},{6,22},{7,23},{8,24},{9,... | collective-permute-start | bytes 1769480 | tf_op jit(solution)/shard_map/ppermute | solution.py:77
  90.3 20.1 %collective-permute-start.22 = (bf16[192,768]{1,0:T(8,128)(2,1)}, bf16[192,768]{1,0:T(8,128)(2,1)S(1)}, u32[]{:S(2)}, u32[]{:S(2)}) collective-permute-start(bf16[192,768]{1,0:T(8,128)(2,1)} %get-tuple-element.138), channel_id=1, source_target_pairs={{0,2},{1,3},{2,0},{3,1},{4,6},{5,7},{6,4},{7,5},{8,10},{9,11},{10,... | collective-permute-start | bytes 884744 | tf_op jit(solution)/shard_map/ppermute | solution.py:77
  91.5 24.6 %collective-permute-start.25 = (bf16[192,768]{1,0:T(8,128)(2,1)}, bf16[192,768]{1,0:T(8,128)(2,1)S(1)}, u32[]{:S(2)}, u32[]{:S(2)}) collective-permute-start(bf16[192,768]{1,0:T(8,128)(2,1)} %get-tuple-element.138), channel_id=1, source_target_pairs={{0,10},{1,11},{2,8},{3,9},{4,14},{5,15},{6,12},{7,13},{8,2},{9,3},... | collective-permute-start | bytes 884744 | tf_op jit(solution)/shard_map/ppermute | solution.py:77
  97.3 24.4 %collective-permute-start.24 = (bf16[192,768]{1,0:T(8,128)(2,1)}, bf16[192,768]{1,0:T(8,128)(2,1)S(1)}, u32[]{:S(2)}, u32[]{:S(2)}) collective-permute-start(bf16[192,768]{1,0:T(8,128)(2,1)} %get-tuple-element.140.refs_6_), channel_id=1, source_target_pairs={{0,8},{1,9},{2,10},{3,11},{4,12},{5,13},{6,14},{7,15},{8,0},{9,1},... | collective-permute-start | bytes 884744 | tf_op jit(solution)/shard_map/ppermute | solution.py:77
  110.4 36.9 %collective-permute-start.20 = (bf16[3,128,768]{2,1,0:T(8,128)(2,1)}, bf16[3,128,768]{2,1,0:T(8,128)(2,1)S(1)}, u32[]{:S(2)}, u32[]{:S(2)}) collective-permute-start(bf16[3,128,768]{2,1,0:T(8,128)(2,1)} %collective-permute-done.19.refs_2_), channel_id=1, source_target_pairs={{0,4},{1,5},{2,6},{3,7},{4,0},{5,1},{6,2},{7,3},{8,12},{9,13},{10,... | collective-permute-start | bytes 1769480 | tf_op jit(solution)/shard_map/ppermute | solution.py:77
  121.8 25.5 %collective-permute-start.26 = (bf16[384,768]{1,0:T(8,128)(2,1)S(1)}, bf16[384,768]{1,0:T(8,128)(2,1)S(1)}, u32[]{:S(2)}, u32[]{:S(2)}) collective-permute-start(bf16[384,768]{1,0:T(8,128)(2,1)S(1)} %pad_maximum_fusion.9), channel_id=1, source_target_pairs={{0,1},{1,0},{2,3},{3,2},{4,5},{5,4},{6,7},{7,6},{8,9},{9,8},{10,11... | collective-permute-start | bytes 1769480 | tf_op jit(solution)/shard_map/ppermute | solution.py:77
  122.4 26.5 %collective-permute-start.23 = (bf16[3,128,768]{2,1,0:T(8,128)(2,1)}, bf16[3,128,768]{2,1,0:T(8,128)(2,1)}, u32[]{:S(2)}, u32[]{:S(2)}) collective-permute-start(bf16[3,128,768]{2,1,0:T(8,128)(2,1)} %collective-permute-done.21.refs_4_), channel_id=1, source_target_pairs={{0,4},{1,5},{2,6},{3,7},{4,0},{5,1},{6,2},{7,3},{8,12},{9,13},{10,... | collective-permute-start | bytes 1769480 | tf_op jit(solution)/shard_map/ppermute | solution.py:77
  123.3 21.0 %collective-permute-start.11 = (bf16[2,73,8,128]{3,2,1,0:T(8,128)(2,1)S(1)}, bf16[2,73,8,128]{3,2,1,0:T(8,128)(2,1)S(1)}, u32[]{:S(2)}, u32[]{:S(2)}) collective-permute-start(bf16[2,73,8,128]{3,2,1,0:T(8,128)(2,1)S(1)} %slice.399), channel_id=1, source_target_pairs={{0,4},{1,5},{2,6},{3,7},{4,0},{5,1},{6,2},{7,3},{8,12},{9,13},{10,... | collective-permute-start | bytes 897032 | tf_op jit(solution)/shard_map/ppermute | solution.py:77
  144.3 14.5 %collective-permute-start.17 = (bf16[4,72,8,128]{3,2,1,0:T(8,128)(2,1)S(1)}, bf16[4,72,8,128]{3,2,1,0:T(8,128)(2,1)}, u32[]{:S(2)}, u32[]{:S(2)}) collective-permute-start(bf16[4,72,8,128]{3,2,1,0:T(8,128)(2,1)S(1)} %pad_maximum_fusion.8), channel_id=1, source_target_pairs={{0,4},{1,5},{2,6},{3,7},{4,0},{5,1},{6,2},{7,3},{8,12},{9,13},{10,... | collective-permute-start | bytes 1769480 | tf_op jit(solution)/shard_map/ppermute | solution.py:77
  145.5 15.5 %collective-permute-start.15 = (bf16[4,73,8,128]{3,2,1,0:T(8,128)(2,1)S(1)}, bf16[4,73,8,128]{3,2,1,0:T(8,128)(2,1)S(1)}, u32[]{:S(2)}, u32[]{:S(2)}) collective-permute-start(bf16[4,73,8,128]{3,2,1,0:T(8,128)(2,1)S(1)} %pad_maximum_fusion.6), channel_id=1, source_target_pairs={{0,2},{1,3},{2,0},{3,1},{4,6},{5,7},{6,4},{7,5},{8,10},{9,11},{10,... | collective-permute-start | bytes 1794056 | tf_op jit(solution)/shard_map/ppermute | solution.py:77
  163.0 17.2 %collective-permute-start.30 = (bf16[192,768]{1,0:T(8,128)(2,1)}, bf16[192,768]{1,0:T(8,128)(2,1)}, u32[]{:S(2)}, u32[]{:S(2)}) collective-permute-start(bf16[192,768]{1,0:T(8,128)(2,1)} %pad_maximum_fusion.19), channel_id=1, source_target_pairs={{0,2},{1,3},{2,0},{3,1},{4,6},{5,7},{6,4},{7,5},{8,10},{9,11},{10,... | collective-permute-start | bytes 884744 | tf_op jit(solution)/shard_map/ppermute | solution.py:77
  164.9 15.3 %collective-permute-start.31 = (bf16[192,768]{1,0:T(8,128)(2,1)}, bf16[192,768]{1,0:T(8,128)(2,1)}, u32[]{:S(2)}, u32[]{:S(2)}) collective-permute-start(bf16[192,768]{1,0:T(8,128)(2,1)} %pad_maximum_fusion.20), channel_id=1, source_target_pairs={{0,8},{1,9},{2,10},{3,11},{4,12},{5,13},{6,14},{7,15},{8,0},{9,1},... | collective-permute-start | bytes 884744 | tf_op jit(solution)/shard_map/ppermute | solution.py:77
  165.6 14.6 %collective-permute-start.32 = (bf16[192,768]{1,0:T(8,128)(2,1)}, bf16[192,768]{1,0:T(8,128)(2,1)}, u32[]{:S(2)}, u32[]{:S(2)}) collective-permute-start(bf16[192,768]{1,0:T(8,128)(2,1)} %pad_maximum_fusion.21), channel_id=1, source_target_pairs={{0,10},{1,11},{2,8},{3,9},{4,14},{5,15},{6,12},{7,13},{8,2},{9,3},... | collective-permute-start | bytes 884744 | tf_op jit(solution)/shard_map/ppermute | solution.py:77
  227.5 41.6 %collective-permute-start.34 = (bf16[3,128,768]{2,1,0:T(8,128)(2,1)S(1)}, bf16[3,128,768]{2,1,0:T(8,128)(2,1)S(1)}, u32[]{:S(2)}, u32[]{:S(2)}) collective-permute-start(bf16[3,128,768]{2,1,0:T(8,128)(2,1)S(1)} %get-tuple-element.161), channel_id=1, source_target_pairs={{0,16},{1,17},{2,18},{3,19},{4,20},{5,21},{6,22},{7,23},{8,24},{9,... | collective-permute-start | bytes 1769480 | tf_op jit(solution)/shard_map/ppermute | solution.py:77
  229.3 52.3 %collective-permute-start.36 = (bf16[3,128,768]{2,1,0:T(8,128)(2,1)S(1)}, bf16[3,128,768]{2,1,0:T(8,128)(2,1)S(1)}, u32[]{:S(2)}, u32[]{:S(2)}) collective-permute-start(bf16[3,128,768]{2,1,0:T(8,128)(2,1)S(1)} %get-tuple-element.164), channel_id=1, source_target_pairs={{0,16},{1,17},{2,18},{3,19},{4,20},{5,21},{6,22},{7,23},{8,24},{9,... | collective-permute-start | bytes 1769480 | tf_op jit(solution)/shard_map/ppermute | solution.py:77
  230.4 57.6 %collective-permute-start.33 = (bf16[3,256,768]{2,1,0:T(8,128)(2,1)S(1)}, bf16[3,256,768]{2,1,0:T(8,128)(2,1)S(1)}, u32[]{:S(2)}, u32[]{:S(2)}) collective-permute-start(bf16[3,256,768]{2,1,0:T(8,128)(2,1)S(1)} %copy-done.3), channel_id=1, source_target_pairs={{0,4},{1,5},{2,6},{3,7},{4,0},{5,1},{6,2},{7,3},{8,12},{9,13},{10,... | collective-permute-start | bytes 3538952 | tf_op jit(solution)/shard_map/ppermute | solution.py:77
  232.1 51.1 %collective-permute-start.44 = (bf16[192,768]{1,0:T(8,128)(2,1)S(1)}, bf16[192,768]{1,0:T(8,128)(2,1)S(1)}, u32[]{:S(2)}, u32[]{:S(2)}) collective-permute-start(bf16[192,768]{1,0:T(8,128)(2,1)S(1)} %copy-done.59), channel_id=1, source_target_pairs={{0,10},{1,11},{2,8},{3,9},{4,14},{5,15},{6,12},{7,13},{8,2},{9,3},... | collective-permute-start | bytes 884744 | tf_op jit(solution)/shard_map/ppermute | solution.py:77
  233.3 50.5 %collective-permute-start.42 = (bf16[192,768]{1,0:T(8,128)(2,1)S(1)}, bf16[192,768]{1,0:T(8,128)(2,1)S(1)}, u32[]{:S(2)}, u32[]{:S(2)}) collective-permute-start(bf16[192,768]{1,0:T(8,128)(2,1)S(1)} %copy-done.59), channel_id=1, source_target_pairs={{0,2},{1,3},{2,0},{3,1},{4,6},{5,7},{6,4},{7,5},{8,10},{9,11},{10,... | collective-permute-start | bytes 884744 | tf_op jit(solution)/shard_map/ppermute | solution.py:77
  269.1 18.8 %collective-permute-start.43 = (bf16[192,768]{1,0:T(8,128)(2,1)S(1)}, bf16[192,768]{1,0:T(8,128)(2,1)S(1)}, u32[]{:S(2)}, u32[]{:S(2)}) collective-permute-start(bf16[192,768]{1,0:T(8,128)(2,1)S(1)} %copy-done.29), channel_id=1, source_target_pairs={{0,8},{1,9},{2,10},{3,11},{4,12},{5,13},{6,14},{7,15},{8,0},{9,1},... | collective-permute-start | bytes 884744 | tf_op jit(solution)/shard_map/ppermute | solution.py:77
  281.7 16.2 %collective-permute-start.35 = (bf16[3,128,768]{2,1,0:T(8,128)(2,1)S(1)}, bf16[3,128,768]{2,1,0:T(8,128)(2,1)S(1)}, u32[]{:S(2)}, u32[]{:S(2)}) collective-permute-start(bf16[3,128,768]{2,1,0:T(8,128)(2,1)S(1)} %collective-permute-done.34.refs_2_), channel_id=1, source_target_pairs={{0,4},{1,5},{2,6},{3,7},{4,0},{5,1},{6,2},{7,3},{8,12},{9,13},{10,... | collective-permute-start | bytes 1769480 | tf_op jit(solution)/shard_map/ppermute | solution.py:77
  283.2 26.2 %collective-permute-start.37 = (bf16[3,128,768]{2,1,0:T(8,128)(2,1)S(1)}, bf16[3,128,768]{2,1,0:T(8,128)(2,1)S(1)}, u32[]{:S(2)}, u32[]{:S(2)}) collective-permute-start(bf16[3,128,768]{2,1,0:T(8,128)(2,1)S(1)} %collective-permute-done.36.refs_4_), channel_id=1, source_target_pairs={{0,4},{1,5},{2,6},{3,7},{4,0},{5,1},{6,2},{7,3},{8,12},{9,13},{10,... | collective-permute-start | bytes 1769480 | tf_op jit(solution)/shard_map/ppermute | solution.py:77
  288.0 22.3 %collective-permute-start.45 = (bf16[384,768]{1,0:T(8,128)(2,1)S(1)}, bf16[384,768]{1,0:T(8,128)(2,1)}, u32[]{:S(2)}, u32[]{:S(2)}) collective-permute-start(bf16[384,768]{1,0:T(8,128)(2,1)S(1)} %pad_maximum_fusion.11), channel_id=1, source_target_pairs={{0,1},{1,0},{2,3},{3,2},{4,5},{5,4},{6,7},{7,6},{8,9},{9,8},{10,11... | collective-permute-start | bytes 1769480 | tf_op jit(solution)/shard_map/ppermute | solution.py:77
  338.1 20.3 %collective-permute-start.54 = (bf16[3,128,768]{2,1,0:T(8,128)(2,1)S(1)}, bf16[3,128,768]{2,1,0:T(8,128)(2,1)S(1)}, u32[]{:S(2)}, u32[]{:S(2)}) collective-permute-start(bf16[3,128,768]{2,1,0:T(8,128)(2,1)S(1)} %copy-done.48), channel_id=1, source_target_pairs={{0,4},{1,5},{2,6},{3,7},{4,0},{5,1},{6,2},{7,3},{8,12},{9,13},{10,... | collective-permute-start | bytes 1769480 | tf_op jit(solution)/shard_map/ppermute | solution.py:77
  339.7 26.4 %collective-permute-start.56 = (bf16[3,128,768]{2,1,0:T(8,128)(2,1)S(1)}, bf16[3,128,768]{2,1,0:T(8,128)(2,1)S(1)}, u32[]{:S(2)}, u32[]{:S(2)}) collective-permute-start(bf16[3,128,768]{2,1,0:T(8,128)(2,1)S(1)} %copy-done.46), channel_id=1, source_target_pairs={{0,4},{1,5},{2,6},{3,7},{4,0},{5,1},{6,2},{7,3},{8,12},{9,13},{10,... | collective-permute-start | bytes 1769480 | tf_op jit(solution)/shard_map/ppermute | solution.py:77
  341.3 16.9 %collective-permute-start.53 = (bf16[192,768]{1,0:T(8,128)(2,1)S(1)}, bf16[192,768]{1,0:T(8,128)(2,1)S(1)}, u32[]{:S(2)}, u32[]{:S(2)}) collective-permute-start(bf16[192,768]{1,0:T(8,128)(2,1)S(1)} %pad_maximum_fusion.29), channel_id=1, source_target_pairs={{0,10},{1,11},{2,8},{3,9},{4,14},{5,15},{6,12},{7,13},{8,2},{9,3},... | collective-permute-start | bytes 884744 | tf_op jit(solution)/shard_map/ppermute | solution.py:77
  349.3 17.8 %collective-permute-start.47 = (bf16[192,768]{1,0:T(8,128)(2,1)S(1)}, bf16[192,768]{1,0:T(8,128)(2,1)S(1)}, u32[]{:S(2)}, u32[]{:S(2)}) collective-permute-start(bf16[192,768]{1,0:T(8,128)(2,1)S(1)} %pad_maximum_fusion.23), channel_id=1, source_target_pairs={{0,2},{1,3},{2,0},{3,1},{4,6},{5,7},{6,4},{7,5},{8,10},{9,11},{10,... | collective-permute-start | bytes 884744 | tf_op jit(solution)/shard_map/ppermute | solution.py:77
  351.0 23.0 %collective-permute-start.48 = (bf16[192,768]{1,0:T(8,128)(2,1)S(1)}, bf16[192,768]{1,0:T(8,128)(2,1)S(1)}, u32[]{:S(2)}, u32[]{:S(2)}) collective-permute-start(bf16[192,768]{1,0:T(8,128)(2,1)S(1)} %pad_maximum_fusion.24), channel_id=1, source_target_pairs={{0,8},{1,9},{2,10},{3,11},{4,12},{5,13},{6,14},{7,15},{8,0},{9,1},... | collective-permute-start | bytes 884744 | tf_op jit(solution)/shard_map/ppermute | solution.py:77
  358.2 20.8 %collective-permute-start.49 = (bf16[192,768]{1,0:T(8,128)(2,1)S(1)}, bf16[192,768]{1,0:T(8,128)(2,1)S(1)}, u32[]{:S(2)}, u32[]{:S(2)}) collective-permute-start(bf16[192,768]{1,0:T(8,128)(2,1)S(1)} %pad_maximum_fusion.25), channel_id=1, source_target_pairs={{0,10},{1,11},{2,8},{3,9},{4,14},{5,15},{6,12},{7,13},{8,2},{9,3},... | collective-permute-start | bytes 884744 | tf_op jit(solution)/shard_map/ppermute | solution.py:77
  358.6 76.1 %collective-permute-start.55 = (bf16[3,128,768]{2,1,0:T(8,128)(2,1)S(1)}, bf16[3,128,768]{2,1,0:T(8,128)(2,1)S(1)}, u32[]{:S(2)}, u32[]{:S(2)}) collective-permute-start(bf16[3,128,768]{2,1,0:T(8,128)(2,1)S(1)} %add_convert_fusion.7), channel_id=1, source_target_pairs={{0,16},{1,17},{2,18},{3,19},{4,20},{5,21},{6,22},{7,23},{8,24},{9,... | collective-permute-start | bytes 1769480 | tf_op jit(solution)/shard_map/ppermute | solution.py:77
  367.1 67.7 %collective-permute-start.57 = (bf16[3,128,768]{2,1,0:T(8,128)(2,1)}, bf16[3,128,768]{2,1,0:T(8,128)(2,1)S(1)}, u32[]{:S(2)}, u32[]{:S(2)}) collective-permute-start(bf16[3,128,768]{2,1,0:T(8,128)(2,1)} %add_convert_fusion.6), channel_id=1, source_target_pairs={{0,16},{1,17},{2,18},{3,19},{4,20},{5,21},{6,22},{7,23},{8,24},{9,... | collective-permute-start | bytes 1769480 | tf_op jit(solution)/shard_map/ppermute | solution.py:77
  367.1 67.7 %collective-permute-start.58 = (bf16[3,256,768]{2,1,0:T(8,128)(2,1)}, bf16[3,256,768]{2,1,0:T(8,128)(2,1)S(1)}, u32[]{:S(2)}, u32[]{:S(2)}) collective-permute-start(bf16[3,256,768]{2,1,0:T(8,128)(2,1)} %get-tuple-element.195), channel_id=1, source_target_pairs={{0,4},{1,5},{2,6},{3,7},{4,0},{5,1},{6,2},{7,3},{8,12},{9,13},{10,... | collective-permute-start | bytes 3538952 | tf_op jit(solution)/shard_map/ppermute | solution.py:77
  450.1 21.3 %collective-permute-start.71 = (bf16[8,72,8,128]{3,2,1,0:T(8,128)(2,1)}, bf16[8,72,8,128]{3,2,1,0:T(8,128)(2,1)}, u32[]{:S(2)}, u32[]{:S(2)}) collective-permute-start(bf16[8,72,8,128]{3,2,1,0:T(8,128)(2,1)} %get-tuple-element.209), channel_id=1, source_target_pairs={{0,1},{1,0},{2,3},{3,2},{4,5},{5,4},{6,7},{7,6},{8,9},{9,8},{10,11... | collective-permute-start | bytes 3538952 | tf_op jit(solution)/shard_map/ppermute | solution.py:77
  450.6 22.8 %collective-permute-start.67 = (bf16[8,73,8,128]{3,2,1,0:T(8,128)(2,1)}, bf16[8,73,8,128]{3,2,1,0:T(8,128)(2,1)}, u32[]{:S(2)}, u32[]{:S(2)}) collective-permute-start(bf16[8,73,8,128]{3,2,1,0:T(8,128)(2,1)} %get-tuple-element.204), channel_id=1, source_target_pairs={{0,1},{1,0},{2,3},{3,2},{4,5},{5,4},{6,7},{7,6},{8,9},{9,8},{10,11... | collective-permute-start | bytes 3588104 | tf_op jit(solution)/shard_map/ppermute | solution.py:77
  475.2 55.6 %collective-permute-start.75 = (bf16[3,128,768]{2,1,0:T(8,128)(2,1)S(1)}, bf16[3,128,768]{2,1,0:T(8,128)(2,1)S(1)}, u32[]{:S(2)}, u32[]{:S(2)}) collective-permute-start(bf16[3,128,768]{2,1,0:T(8,128)(2,1)S(1)} %copy-done.47), channel_id=1, source_target_pairs={{0,4},{1,5},{2,6},{3,7},{4,0},{5,1},{6,2},{7,3},{8,12},{9,13},{10,... | collective-permute-start | bytes 1769480 | tf_op jit(solution)/shard_map/ppermute | solution.py:77
  476.0 56.2 %collective-permute-start.77 = (bf16[3,128,768]{2,1,0:T(8,128)(2,1)S(1)}, bf16[3,128,768]{2,1,0:T(8,128)(2,1)S(1)}, u32[]{:S(2)}, u32[]{:S(2)}) collective-permute-start(bf16[3,128,768]{2,1,0:T(8,128)(2,1)S(1)} %copy-done.45), channel_id=1, source_target_pairs={{0,4},{1,5},{2,6},{3,7},{4,0},{5,1},{6,2},{7,3},{8,12},{9,13},{10,... | collective-permute-start | bytes 1769480 | tf_op jit(solution)/shard_map/ppermute | solution.py:77
  477.3 38.6 %collective-permute-start.72 = (bf16[4,72,8,128]{3,2,1,0:T(8,128)(2,1)S(1)}, bf16[4,72,8,128]{3,2,1,0:T(8,128)(2,1)S(1)}, u32[]{:S(2)}, u32[]{:S(2)}) collective-permute-start(bf16[4,72,8,128]{3,2,1,0:T(8,128)(2,1)S(1)} %get-tuple-element.210), channel_id=1, source_target_pairs={{0,4},{1,5},{2,6},{3,7},{4,0},{5,1},{6,2},{7,3},{8,12},{9,13},{10,... | collective-permute-start | bytes 1769480 | tf_op jit(solution)/shard_map/ppermute | solution.py:77
  478.0 38.3 %collective-permute-start.68 = (bf16[4,73,8,128]{3,2,1,0:T(8,128)(2,1)S(1)}, bf16[4,73,8,128]{3,2,1,0:T(8,128)(2,1)S(1)}, u32[]{:S(2)}, u32[]{:S(2)}) collective-permute-start(bf16[4,73,8,128]{3,2,1,0:T(8,128)(2,1)S(1)} %get-tuple-element.205), channel_id=1, source_target_pairs={{0,2},{1,3},{2,0},{3,1},{4,6},{5,7},{6,4},{7,5},{8,10},{9,11},{10,... | collective-permute-start | bytes 1794056 | tf_op jit(solution)/shard_map/ppermute | solution.py:77
  479.5 40.6 %collective-permute-start.64 = (bf16[192,768]{1,0:T(8,128)(2,1)S(1)}, bf16[192,768]{1,0:T(8,128)(2,1)S(1)}, u32[]{:S(2)}, u32[]{:S(2)}) collective-permute-start(bf16[192,768]{1,0:T(8,128)(2,1)S(1)} %pad_maximum_fusion.31), channel_id=1, source_target_pairs={{0,2},{1,3},{2,0},{3,1},{4,6},{5,7},{6,4},{7,5},{8,10},{9,11},{10,... | collective-permute-start | bytes 884744 | tf_op jit(solution)/shard_map/ppermute | solution.py:77
  516.3 14.4 %collective-permute-start.66 = (bf16[192,768]{1,0:T(8,128)(2,1)S(1)}, bf16[192,768]{1,0:T(8,128)(2,1)S(1)}, u32[]{:S(2)}, u32[]{:S(2)}) collective-permute-start(bf16[192,768]{1,0:T(8,128)(2,1)S(1)} %pad_maximum_fusion.33), channel_id=1, source_target_pairs={{0,10},{1,11},{2,8},{3,9},{4,14},{5,15},{6,12},{7,13},{8,2},{9,3},... | collective-permute-start | bytes 884744 | tf_op jit(solution)/shard_map/ppermute | solution.py:77
  520.1 67.6 %collective-permute-start.73 = (bf16[2,72,8,128]{3,2,1,0:T(8,128)(2,1)S(1)}, bf16[2,72,8,128]{3,2,1,0:T(8,128)(2,1)}, u32[]{:S(2)}, u32[]{:S(2)}) collective-permute-start(bf16[2,72,8,128]{3,2,1,0:T(8,128)(2,1)S(1)} %get-tuple-element.211), channel_id=1, source_target_pairs={{0,2},{1,3},{2,0},{3,1},{4,6},{5,7},{6,4},{7,5},{8,10},{9,11},{10,... | collective-permute-start | bytes 884744 | tf_op jit(solution)/shard_map/ppermute | solution.py:77
  525.8 65.6 %collective-permute-start.69 = (bf16[2,73,8,128]{3,2,1,0:T(8,128)(2,1)}, bf16[2,73,8,128]{3,2,1,0:T(8,128)(2,1)}, u32[]{:S(2)}, u32[]{:S(2)}) collective-permute-start(bf16[2,73,8,128]{3,2,1,0:T(8,128)(2,1)} %get-tuple-element.206), channel_id=1, source_target_pairs={{0,4},{1,5},{2,6},{3,7},{4,0},{5,1},{6,2},{7,3},{8,12},{9,13},{10,... | collective-permute-start | bytes 897032 | tf_op jit(solution)/shard_map/ppermute | solution.py:77
  531.7 58.3 %collective-permute-start.76 = (bf16[3,128,768]{2,1,0:T(8,128)(2,1)}, bf16[3,128,768]{2,1,0:T(8,128)(2,1)}, u32[]{:S(2)}, u32[]{:S(2)}) collective-permute-start(bf16[3,128,768]{2,1,0:T(8,128)(2,1)} %add_convert_fusion.3), channel_id=1, source_target_pairs={{0,16},{1,17},{2,18},{3,19},{4,20},{5,21},{6,22},{7,23},{8,24},{9,... | collective-permute-start | bytes 1769480 | tf_op jit(solution)/shard_map/ppermute | solution.py:77
  533.2 56.9 %collective-permute-start.78 = (bf16[3,128,768]{2,1,0:T(8,128)(2,1)}, bf16[3,128,768]{2,1,0:T(8,128)(2,1)}, u32[]{:S(2)}, u32[]{:S(2)}) collective-permute-start(bf16[3,128,768]{2,1,0:T(8,128)(2,1)} %add_convert_fusion.2), channel_id=1, source_target_pairs={{0,16},{1,17},{2,18},{3,19},{4,20},{5,21},{6,22},{7,23},{8,24},{9,... | collective-permute-start | bytes 1769480 | tf_op jit(solution)/shard_map/ppermute | solution.py:77
  535.7 54.4 %collective-permute-start.79 = (bf16[3,256,768]{2,1,0:T(8,128)(2,1)}, bf16[3,256,768]{2,1,0:T(8,128)(2,1)}, u32[]{:S(2)}, u32[]{:S(2)}) collective-permute-start(bf16[3,256,768]{2,1,0:T(8,128)(2,1)} %get-tuple-element.226), channel_id=1, source_target_pairs={{0,4},{1,5},{2,6},{3,7},{4,0},{5,1},{6,2},{7,3},{8,12},{9,13},{10,... | collective-permute-start | bytes 3538952 | tf_op jit(solution)/shard_map/ppermute | solution.py:77
  (114 other events, 1178.0 us)
